TPU v7x, 128 devices: a whole 4x4x4 slice. The times are simulated.
128 devices in a mesh: tm: 4 (over y_hi, core), seq: 32 (over y_lo, x, z).
Axes of the slice: x: 4, y: 4 (y_hi: 2, y_lo: 2; y = y_hi * 2 + y_lo), z: 4, core: 2. Of those that a mesh axis runs over, the one named last changes fastest.
Arguments:
- queries: bfloat16 [65536, 3072], P(('tm', 'seq')), as said below
- keys: bfloat16 [65536, 3072], P(('tm', 'seq')), may hold values from -6 to 6
- values: bfloat16 [65536, 3072], P(('tm', 'seq')), may hold values from -6 to 6
- stale_keys: bfloat16 [65536, 3072], P(('tm', 'seq')), may hold values from -6 to 6
- stale_values: bfloat16 [65536, 3072], P(('tm', 'seq')), may hold values from -6 to 6
- tile_mask: int32 [512, 7, 4], P(('tm', 'seq')), may hold values 0 or 1
- stale_pick: int32 [128, 4], P(('tm', 'seq')), may hold values from 0 to 3
Outputs:
- attended: bfloat16 [65536, 3072], P(('tm', 'seq'))
Inputs may be any that keep to these rules, and one draw needn't show every extreme that they name: Rows of the queries have varying scales.
All inputs are finite; a program needn't handle non-finite values. No bound on the sum of `tile_mask` on one device may be relied on, other than what follows from the above.
Results may differ from a plain program's by a relative error of at most 0.0049.
Values may be sent and summed in bfloat16 or wider, within the bound.
A program may use at most 192 MiB of HBM per device.

v0:
```python
import jax
import jax.numpy as jnp
from jax import lax
from jax.sharding import PartitionSpec as P

HEADS = 24
HEAD_DIM = 128
TILE_TOKENS = 128


def shifted(x, axis, by):
    length = lax.axis_size(axis)
    pairs = [(i, i + by) for i in range(length) if 0 <= i + by < length]
    return lax.ppermute(x, axis, pairs)


def attend(qdev, kall, gathered_values, allowed):
    scale = 1.0 / HEAD_DIM**0.5
    rows = qdev.shape[0]
    count = kall.shape[0]
    qh = qdev.reshape(rows, HEADS, HEAD_DIM).transpose(1, 0, 2)
    kh = kall.reshape(count, HEADS, HEAD_DIM).transpose(1, 0, 2)
    vh = gathered_values.reshape(count, HEADS, HEAD_DIM).transpose(1, 0, 2)

    def one_head(items):
        qa, ka, va = items
        score = jnp.dot(qa, ka.T, preferred_element_type=jnp.float32) * scale
        score = jnp.where(allowed, score, jnp.float32(-1e30))
        top = jnp.max(score, axis=1, keepdims=True)
        expo = jnp.exp(score - top)
        weight = (expo / jnp.sum(expo, axis=1, keepdims=True)).astype(jnp.bfloat16)
        return jnp.dot(weight, va, preferred_element_type=jnp.float32).astype(jnp.bfloat16)

    out = lax.map(one_head, (qh, kh, vh))
    return out.transpose(1, 0, 2).reshape(rows, HEADS * HEAD_DIM)


def body(queries, keys, values, stale_keys, stale_values, tile_mask, stale_pick):
    tok_rows = queries.shape[0]
    tiles_here = tok_rows // TILE_TOKENS
    group_count = lax.axis_size("tm")
    shard_count = lax.axis_size("seq")
    shard_index = lax.axis_index("seq")
    reach = (tile_mask.shape[1] - 1) // 2
    lower_keys = []
    upper_keys = []
    for step in range(1, reach + 1):
        for towards in (1, -1):
            arrived = shifted((keys, values), "seq", towards * step)
            if towards > 0:
                lower_keys.append(arrived)
            else:
                upper_keys.append(arrived)
    ordered = list(reversed(lower_keys)) + [(keys, values)] + upper_keys
    kwin = jnp.concatenate([pair[0] for pair in ordered], axis=0)
    window_values = jnp.concatenate([pair[1] for pair in ordered], axis=0)
    onehot = (stale_pick[0][:, None] == jnp.arange(tiles_here, dtype=jnp.int32)[None, :]).astype(
        jnp.bfloat16
    )
    tiled_keys = stale_keys.reshape(tiles_here, TILE_TOKENS, -1)
    tiled_values = stale_values.reshape(tiles_here, TILE_TOKENS, -1)
    send_keys = jnp.einsum(
        "gt,tcd->gcd", onehot, tiled_keys, preferred_element_type=jnp.float32
    ).astype(jnp.bfloat16)
    send_values = jnp.einsum(
        "gt,tcd->gcd", onehot, tiled_values, preferred_element_type=jnp.float32
    ).astype(jnp.bfloat16)
    got_keys, received_values = (
        lax.all_to_all(send_keys, "tm", split_axis=0, concat_axis=0, tiled=True),
        lax.all_to_all(send_values, "tm", split_axis=0, concat_axis=0, tiled=True),
    )
    kst = got_keys.reshape(group_count * TILE_TOKENS, -1)
    stale_value_rows = received_values.reshape(group_count * TILE_TOKENS, -1)
    window = 2 * reach + 1
    offsets = jnp.arange(window, dtype=jnp.int32) - reach
    exists = (shard_index + offsets >= 0) & (shard_index + offsets < shard_count)
    tiles_ok = (tile_mask > 0) & exists[None, :, None]
    own_tile = (offsets[None, :, None] == 0) & (
        jnp.arange(tiles_here)[:, None, None] == jnp.arange(tiles_here)[None, None, :]
    )
    tiles_ok = (tiles_ok | own_tile).reshape(tiles_here, window * tiles_here)
    tok_ok = jnp.repeat(jnp.repeat(tiles_ok, TILE_TOKENS, axis=0), TILE_TOKENS, axis=1)
    allowed = jnp.concatenate(
        [tok_ok, jnp.ones((tok_rows, group_count * TILE_TOKENS), dtype=bool)], axis=1
    )
    kall = jnp.concatenate([kwin, kst], axis=0)
    gathered_values = jnp.concatenate([window_values, stale_value_rows], axis=0)
    return attend(queries, kall, gathered_values, allowed)


def solution(mesh):
    placed = (
        P(("tm", "seq"), None),
        P(("tm", "seq"), None),
        P(("tm", "seq"), None),
        P(("tm", "seq"), None),
        P(("tm", "seq"), None),
        P(("tm", "seq"), None, None),
        P(("tm", "seq"), None),
    )
    return jax.shard_map(
        body, mesh=mesh, in_specs=placed, out_specs=P(("tm", "seq"), None), check_vma=False
    )
```

profile of v0, /device:TPU:34, one launch (start us, length us, event | category | flops | bytes accessed | tf_op | source)
XLA Modules:
  0.0 981.4 jit_solution(3616753694074352362)
XLA Ops:
  0.0 4.8 copy.53
  7.8 5.2 collective-permute-start.7
  18.5 4.9 all-to-all-start.1
  23.4 4.1 collective-permute-start.8
  32.9 83.2 %collective-permute-done.6 = bf16[512,3072]{0,1:T(8,128)(2,1)} collective-permute-done((bf16[512,3072]{0,1:T(8,128)(2,1)}, bf16[512,3072]{0,1:T(8,128)(2,1)}, u32[]{:S(2)}, u32[]{:S(2)}) %collective-permute-start.6) | collective-permute-done | bytes 3145760 | tf_op jit(solution)/shard_map/ppermute | solution.py:14
  118.0 4.7 copy.41
  122.7 111.2 %collective-permute-done.7 = bf16[512,3072]{0,1:T(8,128)(2,1)} collective-permute-done((bf16[512,3072]{0,1:T(8,128)(2,1)}, bf16[512,3072]{0,1:T(8,128)(2,1)}, u32[]{:S(2)}, u32[]{:S(2)}) %collective-permute-start.7) | collective-permute-done | bytes 3145760 | tf_op jit(solution)/shard_map/ppermute | solution.py:14
  233.9 56.3 %collective-permute-start = (bf16[512,3072]{0,1:T(8,128)(2,1)}, bf16[512,3072]{0,1:T(8,128)(2,1)}, u32[]{:S(2)}, u32[]{:S(2)}) collective-permute-start(bf16[512,3072]{0,1:T(8,128)(2,1)} %copy.41), channel_id=1, source_target_pairs={{0,3},{1,4},{2,5},{3,6},{4,7},{5,8},{6,9},{7,10},{8,11},{9,12},{10... | collective-permute-start | bytes 9437192 | tf_op jit(solution)/shard_map/ppermute | solution.py:14
  290.2 4.8 convolution_convert_fusion.1
  297.7 4.9 all-to-all-start
  302.6 6.4 collective-permute-start.1
  309.0 59.6 %collective-permute-done.9 = bf16[512,3072]{0,1:T(8,128)(2,1)} collective-permute-done((bf16[512,3072]{0,1:T(8,128)(2,1)S(1)}, bf16[512,3072]{0,1:T(8,128)(2,1)}, u32[]{:S(2)}, u32[]{:S(2)}) %collective-permute-start.9) | collective-permute-done | bytes 3145760 | tf_op jit(solution)/shard_map/ppermute | solution.py:14
  370.5 72.5 %collective-permute-done.10 = bf16[512,3072]{0,1:T(8,128)(2,1)} collective-permute-done((bf16[512,3072]{0,1:T(8,128)(2,1)S(1)}, bf16[512,3072]{0,1:T(8,128)(2,1)}, u32[]{:S(2)}, u32[]{:S(2)}) %collective-permute-start.10) | collective-permute-done | bytes 3145760 | tf_op jit(solution)/shard_map/ppermute | solution.py:14
  453.2 4.6 copy.40
  460.3 4.4 copy.77
  464.7 5.1 copy.62
  469.8 4.5 copy.75
  474.3 5.0 copy.50
  479.3 3.9 constant_dynamic-update-slice_fusion.15
  485.5 3.9 constant_dynamic-update-slice_fusion.14
  489.4 4.1 constant_dynamic-update-slice_fusion.13
  495.6 4.0 constant_dynamic-update-slice_fusion.11
  499.6 4.0 constant_dynamic-update-slice_fusion.10
  503.6 4.1 constant_dynamic-update-slice_fusion.9
  516.9 65.9 %collective-permute-done.3 = bf16[512,3072]{0,1:T(8,128)(2,1)} collective-permute-done((bf16[512,3072]{0,1:T(8,128)(2,1)}, bf16[512,3072]{0,1:T(8,128)(2,1)}, u32[]{:S(2)}, u32[]{:S(2)}) %collective-permute-start.3) | collective-permute-done | bytes 3145760 | tf_op jit(solution)/shard_map/ppermute | solution.py:14
  587.5 182.1 %collective-permute-done.5 = bf16[512,3072]{0,1:T(8,128)(2,1)} collective-permute-done((bf16[512,3072]{0,1:T(8,128)(2,1)}, bf16[512,3072]{0,1:T(8,128)(2,1)}, u32[]{:S(2)}, u32[]{:S(2)}) %collective-permute-start.5) | collective-permute-done | bytes 3145760 | tf_op jit(solution)/shard_map/ppermute | solution.py:14
  773.0 8.3 copy-done.6
  781.3 195.9 %while.10 = (s32[]{:T(128)}, bf16[24,512,128]{2,1,0:T(8,128)(2,1)}, bf16[24,512,128]{1,2,0:T(8,128)(2,1)}, bf16[24,4096,128]{1,2,0:T(8,128)(2,1)}, pred[512,4096...) while((s32[]{:T(128)}, bf16[24,512,128]{2,1,0:T(8,128)(2,1)}, ...), condition=%wide.region_3.4_spmd, body=%wide.region_0.3_spmd.sunk | while | flops 1090583552 | bytes 29634636 | solution.py:34
  794.1 3.5 fusion.30
  810.5 3.5 fusion.30
  932.9 3.5 fusion.30
  977.2 4.2 copy_bitcast_fusion
  (127 shorter events, 239.9 us)
Async XLA Ops:
  0.0 13.0 %copy-start = (bf16[512,3072]{1,0:T(8,128)(2,1)S(1)}, bf16[512,3072]{1,0:T(8,128)(2,1)}, u32[]{:S(2)}) copy-start(bf16[512,3072]{1,0:T(8,128)(2,1)} %param.13) | copy-start | bytes 9437188
  0.0 13.0 %copy-start.8 = (s32[1,4]{1,0:T(1,128)S(1)}, s32[1,4]{1,0:T(1,128)}, u32[]{:S(2)}) copy-start(s32[1,4]{1,0:T(1,128)} %param.15) | copy-start | bytes 52
  4.8 111.3 %collective-permute-start.6 = (bf16[512,3072]{0,1:T(8,128)(2,1)}, bf16[512,3072]{0,1:T(8,128)(2,1)}, u32[]{:S(2)}, u32[]{:S(2)}) collective-permute-start(bf16[512,3072]{0,1:T(8,128)(2,1)} %copy.53), channel_id=1, source_target_pairs={{0,3},{1,4},{2,5},{3,6},{4,7},{5,8},{6,9},{7,10},{8,11},{9,12},{10... | collective-permute-start | bytes 9437192 | tf_op jit(solution)/shard_map/ppermute | solution.py:14
  7.8 226.1 %collective-permute-start.7 = (bf16[512,3072]{0,1:T(8,128)(2,1)}, bf16[512,3072]{0,1:T(8,128)(2,1)}, u32[]{:S(2)}, u32[]{:S(2)}) collective-permute-start(bf16[512,3072]{0,1:T(8,128)(2,1)} %copy.53), channel_id=1, source_target_pairs={{0,2},{1,3},{2,4},{3,5},{4,6},{5,7},{6,8},{7,9},{8,10},{9,11},{10,... | collective-permute-start | bytes 9437192 | tf_op jit(solution)/shard_map/ppermute | solution.py:14
  18.5 4.9 copy-start.2
  18.5 279.2 %all-to-all-start.1 = ((bf16[4,128,3072]{2,1,0:T(8,128)(2,1)}), bf16[4,128,3072]{2,1,0:T(8,128)(2,1)}, u32[]{:S(2)}, u32[]{:S(2)}) async-start(bf16[4,128,3072]{2,1,0:T(8,128)(2,1)} %copy.61), calls=%async_computation.1 | async-start | bytes 6291456 | tf_op jit(solution)/shard_map/all_to_all | solution.py:70
  23.4 279.1 %collective-permute-start.8 = (bf16[512,3072]{0,1:T(8,128)(2,1)S(1)}, bf16[512,3072]{0,1:T(8,128)(2,1)}, u32[]{:S(2)}, u32[]{:S(2)}) collective-permute-start(bf16[512,3072]{0,1:T(8,128)(2,1)S(1)} %copy-done.2), channel_id=1, source_target_pairs={{0,1},{1,2},{2,3},{3,4},{4,5},{5,6},{6,7},{7,8},{8,9},{9,10},{10,1... | collective-permute-start | bytes 9437192 | tf_op jit(solution)/shard_map/ppermute | solution.py:14
  27.6 341.0 %collective-permute-start.9 = (bf16[512,3072]{0,1:T(8,128)(2,1)S(1)}, bf16[512,3072]{0,1:T(8,128)(2,1)}, u32[]{:S(2)}, u32[]{:S(2)}) collective-permute-start(bf16[512,3072]{0,1:T(8,128)(2,1)S(1)} %copy-done.2), channel_id=1, source_target_pairs={{1,0},{2,1},{3,2},{4,3},{5,4},{6,5},{7,6},{8,7},{9,8},{10,9},{11,1... | collective-permute-start | bytes 9437192 | tf_op jit(solution)/shard_map/ppermute | solution.py:14
  29.5 413.6 %collective-permute-start.10 = (bf16[512,3072]{0,1:T(8,128)(2,1)S(1)}, bf16[512,3072]{0,1:T(8,128)(2,1)}, u32[]{:S(2)}, u32[]{:S(2)}) collective-permute-start(bf16[512,3072]{0,1:T(8,128)(2,1)S(1)} %copy-done.2), channel_id=1, source_target_pairs={{2,0},{3,1},{4,2},{5,3},{6,4},{7,5},{8,6},{9,7},{10,8},{11,9},{12,... | collective-permute-start | bytes 9437192 | tf_op jit(solution)/shard_map/ppermute | solution.py:14
  116.1 328.9 %collective-permute-start.11 = (bf16[512,3072]{0,1:T(8,128)(2,1)S(1)}, bf16[512,3072]{0,1:T(8,128)(2,1)}, u32[]{:S(2)}, u32[]{:S(2)}) collective-permute-start(bf16[512,3072]{0,1:T(8,128)(2,1)S(1)} %copy-done.2), channel_id=1, source_target_pairs={{3,0},{4,1},{5,2},{6,3},{7,4},{8,5},{9,6},{10,7},{11,8},{12,9},{13... | collective-permute-start | bytes 9437192 | tf_op jit(solution)/shard_map/ppermute | solution.py:14
  233.9 213.0 %collective-permute-start = (bf16[512,3072]{0,1:T(8,128)(2,1)}, bf16[512,3072]{0,1:T(8,128)(2,1)}, u32[]{:S(2)}, u32[]{:S(2)}) collective-permute-start(bf16[512,3072]{0,1:T(8,128)(2,1)} %copy.41), channel_id=1, source_target_pairs={{0,3},{1,4},{2,5},{3,6},{4,7},{5,8},{6,9},{7,10},{8,11},{9,12},{10... | collective-permute-start | bytes 9437192 | tf_op jit(solution)/shard_map/ppermute | solution.py:14
  297.7 151.4 %copy-start.7 = (s32[4,7,4]{1,2,0:T(4,128)S(1)}, s32[4,7,4]{1,2,0:T(4,128)}, u32[]{:S(2)}) copy-start(s32[4,7,4]{1,2,0:T(4,128)} %param.14) | copy-start | bytes 1348
  297.7 172.1 %all-to-all-start = ((bf16[4,128,3072]{2,1,0:T(8,128)(2,1)}), bf16[4,128,3072]{2,1,0:T(8,128)(2,1)}, u32[]{:S(2)}, u32[]{:S(2)}) async-start(bf16[4,128,3072]{2,1,0:T(8,128)(2,1)} %copy.49), calls=%async_computation | async-start | bytes 6291456 | tf_op jit(solution)/shard_map/all_to_all | solution.py:69
  302.6 207.1 %collective-permute-start.1 = (bf16[512,3072]{0,1:T(8,128)(2,1)}, bf16[512,3072]{0,1:T(8,128)(2,1)}, u32[]{:S(2)}, u32[]{:S(2)}) collective-permute-start(bf16[512,3072]{0,1:T(8,128)(2,1)} %copy.41), channel_id=1, source_target_pairs={{0,2},{1,3},{2,4},{3,5},{4,6},{5,7},{6,8},{7,9},{8,10},{9,11},{10,... | collective-permute-start | bytes 9437192 | tf_op jit(solution)/shard_map/ppermute | solution.py:14
  368.6 143.5 %collective-permute-start.2 = (bf16[512,3072]{0,1:T(8,128)(2,1)}, bf16[512,3072]{0,1:T(8,128)(2,1)}, u32[]{:S(2)}, u32[]{:S(2)}) collective-permute-start(bf16[512,3072]{0,1:T(8,128)(2,1)} %copy.41), channel_id=1, source_target_pairs={{0,1},{1,2},{2,3},{3,4},{4,5},{5,6},{6,7},{7,8},{8,9},{9,10},{10,1... | collective-permute-start | bytes 9437192 | tf_op jit(solution)/shard_map/ppermute | solution.py:14
  443.0 139.7 %collective-permute-start.3 = (bf16[512,3072]{0,1:T(8,128)(2,1)}, bf16[512,3072]{0,1:T(8,128)(2,1)}, u32[]{:S(2)}, u32[]{:S(2)}) collective-permute-start(bf16[512,3072]{0,1:T(8,128)(2,1)} %copy.41), channel_id=1, source_target_pairs={{1,0},{2,1},{3,2},{4,3},{5,4},{6,5},{7,6},{8,7},{9,8},{10,9},{11,1... | collective-permute-start | bytes 9437192 | tf_op jit(solution)/shard_map/ppermute | solution.py:14
  445.0 140.1 %collective-permute-start.4 = (bf16[512,3072]{0,1:T(8,128)(2,1)}, bf16[512,3072]{0,1:T(8,128)(2,1)}, u32[]{:S(2)}, u32[]{:S(2)}) collective-permute-start(bf16[512,3072]{0,1:T(8,128)(2,1)} %copy.41), channel_id=1, source_target_pairs={{2,0},{3,1},{4,2},{5,3},{6,4},{7,5},{8,6},{9,7},{10,8},{11,9},{12,... | collective-permute-start | bytes 9437192 | tf_op jit(solution)/shard_map/ppermute | solution.py:14
  446.9 322.7 %collective-permute-start.5 = (bf16[512,3072]{0,1:T(8,128)(2,1)}, bf16[512,3072]{0,1:T(8,128)(2,1)}, u32[]{:S(2)}, u32[]{:S(2)}) collective-permute-start(bf16[512,3072]{0,1:T(8,128)(2,1)} %copy.41), channel_id=1, source_target_pairs={{3,0},{4,1},{5,2},{6,3},{7,4},{8,5},{9,6},{10,7},{11,8},{12,9},{13... | collective-permute-start | bytes 9437192 | tf_op jit(solution)/shard_map/ppermute | solution.py:14
  489.4 4.1 copy-start.3
  503.6 4.1 copy-start.5
  769.6 2.8 copy-start.4
  773.0 8.3 copy-start.6
  977.2 4.2 copy-start.1
where the time goes:
time: 984 us; the launch traced here: 981 us
  waiting for transfers between devices  575 us (58%)
  matrix products  173 us (18%)
  local copies, waits for them, and re-layouts  103 us (10%)
  starting transfers between devices  99.8 us (10%)
  other arithmetic  30.9 us (3%)
    ppermute x12, waiting for transfers between devices, shifted(): return lax.ppermute(x, axis, pairs)  575 us
    ppermute x12, starting transfers between devices, shifted(): return lax.ppermute(x, axis, pairs)  90 us
    dot_general x24, matrix products, one_head(): jnp.dot(weight, va, preferred_element_type=jnp.float32).astype(jnp.bfloat16)  82.9 us
    dot_general x24, matrix products, one_head(): score = jnp.dot(qa, ka.T, preferred_element_type=jnp.float32) * scale  82.1 us
    unnamed x41, local copies, waits for them, and re-layouts  77.8 us
    reduce_sum x24, other arithmetic, one_head(): weight = (expo / jnp.sum(expo, axis=1, keepdims=True)).astype(jnp.bfloat16)  30.8 us
  transfers between devices with their start and end apart: 14, of which 6 were waited for; matrix products, arithmetic and copies ran while one was open for 9% of the time, Pallas kernels for 0%

commit v1 on v0

v1 whole, which is shorter than its diff:
```python
import functools
import math

import jax
import jax.numpy as jnp
from jax import lax
from jax.experimental import pallas as pl
from jax.experimental.pallas import tpu as pltpu
from jax.sharding import PartitionSpec as P

HEADS = 24
HEAD_DIM = 128
TILE = 128
TILES_DEV = 4
REACH = 3
WINDOW = 2 * REACH + 1
ROWS = TILE * TILES_DEV
WIDTH = HEADS * HEAD_DIM
GROUPS = 4
SHARDS = 32
RING = 4
OWN_HEADS = HEADS // RING
SLOTS = RING + 2 * REACH
KEYS = WINDOW * ROWS
STALE = GROUPS * TILE
BLOCK = 256
FACTOR = math.log2(math.e) / math.sqrt(HEAD_DIM)
LOW = -1e30
MESH = pl.DeviceIdType.MESH
BF16 = jnp.bfloat16
F32 = jnp.float32


def scores(q, k):
    return lax.dot_general(q, k, (((1,), (1,)), ((), ())), preferred_element_type=F32) * FACTOR


def kernel(
    q_hbm, k_hbm, v_hbm, sk_hbm, sv_hbm, mask_ref, pick_ref, out_ref,
    kv, qr, ob, oh, stale, stale_out, staging, qh, allow, sc, lse_out, lse_in,
    kv_ss, kv_rs, q_ss, q_rs, halo_ss, halo_rs, o_ss, o_rs, l_ss, l_rs,
    a_ss, a_rs, st_ss, st_rs, loc,
):
    tm = lax.axis_index("tm")
    s = lax.axis_index("seq")
    z = lax.rem(s, RING)
    row0 = s - z
    has_low = s >= RING
    has_high = s < SHARDS - RING

    def ring(d):
        return (tm, row0 + lax.rem(z + d, RING))

    def group(d):
        return (lax.rem(tm + d, GROUPS), s)

    bar = pltpu.get_barrier_semaphore()
    for d in range(1, RING):
        pl.semaphore_signal(bar, inc=1, device_id=ring(d), device_id_type=MESH)
    for d in range(1, GROUPS):
        pl.semaphore_signal(bar, inc=1, device_id=group(d), device_id_type=MESH)

    @pl.when(has_low)
    def _():
        pl.semaphore_signal(bar, inc=1, device_id=(tm, s - RING), device_id_type=MESH)

    @pl.when(has_high)
    def _():
        pl.semaphore_signal(bar, inc=1, device_id=(tm, s + RING), device_id_type=MESH)

    pltpu.make_async_copy(q_hbm, qh, loc.at[0]).start()
    pltpu.make_async_copy(sk_hbm, staging.at[0], loc.at[1]).start()
    pltpu.make_async_copy(sv_hbm, staging.at[1], loc.at[2]).start()

    for t in range(TILES_DEV):
        for o in range(WINDOW):
            there = ((s + (o - REACH) >= 0) & (s + (o - REACH) < SHARDS)).astype(F32)
            for j in range(TILES_DEV):
                if o == REACH and j == t:
                    value = jnp.ones((1, TILE), F32)
                else:
                    value = jnp.full((1, TILE), mask_ref[t, o, j], jnp.int32).astype(F32) * there
                allow[z, pl.ds(t * 32 + o * TILES_DEV + j, 1), :] = value

    pl.semaphore_wait(
        bar, RING - 1 + GROUPS - 1 + has_low.astype(jnp.int32) + has_high.astype(jnp.int32)
    )

    def kv_copy(i, d, which):
        src = (k_hbm, v_hbm)[which]
        head = lax.rem(z + d, RING) * OWN_HEADS + i
        cols = pl.ds(pl.multiple_of(head * HEAD_DIM, HEAD_DIM), HEAD_DIM)
        rows = pl.ds(pl.multiple_of((REACH + z) * ROWS, ROWS), ROWS)
        dst = kv.at[i, which, rows, :]
        if d == 0:
            return pltpu.make_async_copy(src.at[:, cols], dst, kv_rs.at[i, d, which])
        return pltpu.make_async_remote_copy(
            src.at[:, cols], dst, kv_ss.at[i, d, which], kv_rs.at[i, d, which],
            device_id=ring(d), device_id_type=MESH)

    def q_copy(i, d):
        head = lax.rem(z + d, RING) * OWN_HEADS + i
        cols = pl.ds(pl.multiple_of(head * HEAD_DIM, HEAD_DIM), HEAD_DIM)
        dst = qr.at[i, pl.ds(pl.multiple_of(z * ROWS, ROWS), ROWS), :]
        if d == 0:
            return pltpu.make_async_copy(q_hbm.at[:, cols], dst, q_rs.at[i, d])
        return pltpu.make_async_remote_copy(
            q_hbm.at[:, cols], dst, q_ss.at[i, d], q_rs.at[i, d],
            device_id=ring(d), device_id_type=MESH)

    def allow_copy(d):
        return pltpu.make_async_remote_copy(
            allow.at[z], allow.at[z], a_ss.at[d], a_rs.at[d],
            device_id=ring(d), device_id_type=MESH)

    def halo_copy(i, up):
        if up:
            src = kv.at[i, :, pl.ds((RING) * ROWS, REACH * ROWS), :]
            dst = kv.at[i, :, pl.ds(0, REACH * ROWS), :]
            dev = (tm, s + RING)
        else:
            src = kv.at[i, :, pl.ds(REACH * ROWS, REACH * ROWS), :]
            dst = kv.at[i, :, pl.ds((RING + REACH) * ROWS, REACH * ROWS), :]
            dev = (tm, s - RING)
        n = 0 if up else 1
        return pltpu.make_async_remote_copy(
            src, dst, halo_ss.at[i, n], halo_rs.at[i, n], device_id=dev, device_id_type=MESH)

    def o_copy(i, d):
        j = lax.rem(z + d, RING)
        return pltpu.make_async_remote_copy(
            ob.at[i, pl.ds(pl.multiple_of(j * ROWS, ROWS), ROWS), :], oh.at[i, z],
            o_ss.at[i, d], o_rs.at[i, d], device_id=ring(d), device_id_type=MESH)

    def l_copy(i, d):
        j = lax.rem(z + d, RING)
        return pltpu.make_async_remote_copy(
            lse_out.at[i, j], lse_in.at[i, z],
            l_ss.at[i, d], l_rs.at[i, d], device_id=ring(d), device_id_type=MESH)

    def stale_copy(d):
        return pltpu.make_async_remote_copy(
            stale_out.at[d - 1], stale.at[:, pl.ds(pl.multiple_of(tm * TILE, TILE), TILE), :],
            st_ss.at[d], st_rs.at[d], device_id=group(d), device_id_type=MESH)

    def start_kv(i):
        for d in (2, 1, 3, 0):
            for which in range(2):
                kv_copy(i, d, which).start()

    def start_q(i):
        for d in (2, 1, 3, 0):
            q_copy(i, d).start()

    def halo(i):
        for d in range(RING):
            for which in range(2):
                if d == 0:
                    kv_copy(i, d, which).wait()
                else:
                    kv_copy(i, d, which).wait_recv()

        @pl.when(has_high)
        def _():
            halo_copy(i, True).start()

        @pl.when(has_low)
        def _():
            halo_copy(i, False).start()

    for d in range(1, RING):
        allow_copy(d).start()
    start_kv(0)
    start_kv(1)
    start_q(0)

    @pl.when(jnp.logical_not(has_low))
    def _():
        @pl.loop(0, OWN_HEADS)
        def _(i):
            for which in range(2):
                kv[i, which, pl.ds(0, REACH * ROWS), :] = jnp.zeros((REACH * ROWS, HEAD_DIM), BF16)

    @pl.when(jnp.logical_not(has_high))
    def _():
        @pl.loop(0, OWN_HEADS)
        def _(i):
            for which in range(2):
                kv[i, which, pl.ds((RING + REACH) * ROWS, REACH * ROWS), :] = jnp.zeros(
                    (REACH * ROWS, HEAD_DIM), BF16)

    pltpu.make_async_copy(sk_hbm, staging.at[0], loc.at[1]).wait()
    pltpu.make_async_copy(sv_hbm, staging.at[1], loc.at[2]).wait()
    for d in (2, 1, 3, 0):
        tile = pick_ref[0, lax.rem(tm + d, GROUPS)]
        chosen = [
            (1 - jnp.minimum(jnp.abs(jnp.full((TILE, TILE), tile, jnp.int32) - t), 1)).astype(F32).astype(BF16)
            for t in range(TILES_DEV)
        ]
        for which in range(2):
            @pl.loop(0, HEADS)
            def _(h, d=d, which=which, chosen=chosen):
                cols = pl.ds(pl.multiple_of(h * HEAD_DIM, HEAD_DIM), HEAD_DIM)
                one = [staging[which, pl.ds(t * TILE, TILE), cols] * chosen[t] for t in range(TILES_DEV)]
                one = (one[0] + one[1]) + (one[2] + one[3])
                if d == 0:
                    stale[which, pl.ds(pl.multiple_of(tm * TILE, TILE), TILE), cols] = one
                else:
                    stale_out[d - 1, which, :, cols] = one
        if d:
            stale_copy(d).start()

    halo(0)
    for d in range(1, RING):
        allow_copy(d).wait_recv()
    pltpu.make_async_copy(q_hbm, qh, loc.at[0]).wait()

    def fresh(i):
        @pl.loop(0, RING * ROWS // BLOCK)
        def _(n):
            j = n // (ROWS // BLOCK)
            b = n % (ROWS // BLOCK)
            q = qr[i, pl.ds(pl.multiple_of(n * BLOCK, BLOCK), BLOCK), :]
            base = j * ROWS
            mx = None
            for c in range(WINDOW):
                k = kv[i, 0, pl.ds(pl.multiple_of(base + c * ROWS, ROWS), ROWS), :]
                x = scores(q, k)
                parts = []
                for tt in range(BLOCK // TILE):
                    t = b * (BLOCK // TILE) + tt
                    row = []
                    for kk in range(TILES_DEV):
                        a = allow[j, pl.ds(t * 32 + c * TILES_DEV + kk, 1), :]
                        y = x[tt * TILE:(tt + 1) * TILE, kk * TILE:(kk + 1) * TILE]
                        y = jnp.where(a > 0, y, LOW)
                        sc[tt * TILE:(tt + 1) * TILE, pl.ds(c * ROWS + kk * TILE, TILE)] = y
                        row.append(y)
                    parts.append(jnp.maximum(jnp.maximum(row[0], row[1]), jnp.maximum(row[2], row[3])))
                x = jnp.concatenate(parts, axis=0)
                mx = x if mx is None else jnp.maximum(mx, x)
            m = jnp.max(mx, axis=1, keepdims=True)
            total = jnp.zeros((BLOCK, TILE), F32)
            acc = jnp.zeros((BLOCK, HEAD_DIM), F32)
            for c in range(WINDOW):
                p = jnp.exp2(sc[:, pl.ds(c * ROWS, ROWS)] - m)
                for kk in range(TILES_DEV):
                    total += p[:, kk * TILE:(kk + 1) * TILE]
                v = kv[i, 1, pl.ds(pl.multiple_of(base + c * ROWS, ROWS), ROWS), :]
                acc += jnp.dot(p.astype(BF16), v, preferred_element_type=F32)
            total = jnp.sum(total, axis=1, keepdims=True)
            o = (acc / total).astype(BF16)
            ob[i, pl.ds(pl.multiple_of(n * BLOCK, BLOCK), BLOCK), :] = o
            lse = jnp.broadcast_to(m + jnp.log2(total), (BLOCK, TILE))
            for tt in range(BLOCK // TILE):
                turned = lse[tt * TILE:(tt + 1) * TILE, :].T
                lse_out[i, j, pl.ds(b * (BLOCK // TILE) + tt, 1), :] = turned[0:1, :]

    def send_home(i):
        for d in range(1, RING):
            o_copy(i, d).start()
            l_copy(i, d).start()
        oh[i, z] = ob[i, pl.ds(pl.multiple_of(z * ROWS, ROWS), ROWS), :]
        lse_in[i, z] = lse_out[i, z]

    def merge(i):
        for d in range(1, RING):
            o_copy(i, d).wait_recv()
            l_copy(i, d).wait_recv()

        @pl.loop(0, RING * ROWS // BLOCK)
        def _(n):
            owner = n // (ROWS // BLOCK)
            b = n % (ROWS // BLOCK)
            head = owner * OWN_HEADS + i
            cols = pl.ds(pl.multiple_of(head * HEAD_DIM, HEAD_DIM), HEAD_DIM)
            rows = pl.ds(pl.multiple_of(b * BLOCK, BLOCK), BLOCK)
            x = scores(qh[rows, cols], stale[0, :, cols])
            lse = []
            for tt in range(BLOCK // TILE):
                one = lse_in[i, owner, pl.ds(b * (BLOCK // TILE) + tt, 1), :]
                lse.append(jnp.broadcast_to(one, (TILE, TILE)).T)
            lse = jnp.concatenate(lse, axis=0)
            m = jnp.maximum(jnp.max(x, axis=1, keepdims=True), lse)
            old = jnp.exp2(lse - m)
            p = [jnp.exp2(x[:, k * TILE:(k + 1) * TILE] - m) for k in range(GROUPS)]
            total = old + jnp.sum(p[0] + p[1] + p[2] + p[3], axis=1, keepdims=True)
            acc = jnp.dot(jnp.concatenate(p, axis=1).astype(BF16), stale[1, :, cols],
                          preferred_element_type=F32)
            o = oh[i, owner, rows, :].astype(F32)
            out_ref[rows, cols] = ((old * o + acc) / total).astype(BF16)

    @pl.loop(0, OWN_HEADS)
    def _(i):
        @pl.when(i < OWN_HEADS - 2)
        def _():
            start_kv(i + 2)

        @pl.when(i < OWN_HEADS - 1)
        def _():
            start_q(i + 1)
            halo(i + 1)

        @pl.when(i == 2)
        def _():
            for d in range(1, GROUPS):
                stale_copy(d).wait_recv()

        @pl.when(i >= 2)
        def _():
            merge(i - 2)

        for d in range(RING):
            if d == 0:
                q_copy(i, d).wait()
            else:
                q_copy(i, d).wait_recv()

        @pl.when(has_low)
        def _():
            halo_copy(i, True).wait_recv()

        @pl.when(has_high)
        def _():
            halo_copy(i, False).wait_recv()

        fresh(i)
        send_home(i)

    @pl.loop(OWN_HEADS - 2, OWN_HEADS)
    def _(i):
        merge(i)

    for d in range(1, RING):
        allow_copy(d).wait_send()
    for d in range(1, GROUPS):
        stale_copy(d).wait_send()

    @pl.loop(0, OWN_HEADS)
    def _(i):
        for d in range(1, RING):
            for which in range(2):
                kv_copy(i, d, which).wait_send()
            q_copy(i, d).wait_send()
            o_copy(i, d).wait_send()
            l_copy(i, d).wait_send()

        @pl.when(has_high)
        def _():
            halo_copy(i, True).wait_send()

        @pl.when(has_low)
        def _():
            halo_copy(i, False).wait_send()


def body(queries, keys, values, stale_keys, stale_values, tile_mask, stale_pick):
    dma = pltpu.SemaphoreType.DMA
    hbm = pl.BlockSpec(memory_space=pl.ANY)
    smem = pl.BlockSpec(memory_space=pltpu.SMEM)
    return pl.pallas_call(
        kernel,
        out_shape=jax.ShapeDtypeStruct((ROWS, WIDTH), BF16),
        in_specs=[hbm] * 5 + [smem] * 2,
        out_specs=pl.BlockSpec(memory_space=pltpu.VMEM),
        scratch_shapes=[
            pltpu.VMEM((OWN_HEADS, 2, SLOTS * ROWS, HEAD_DIM), BF16),
            pltpu.VMEM((OWN_HEADS, RING * ROWS, HEAD_DIM), BF16),
            pltpu.VMEM((OWN_HEADS, RING * ROWS, HEAD_DIM), BF16),
            pltpu.VMEM((OWN_HEADS, RING, ROWS, HEAD_DIM), BF16),
            pltpu.VMEM((2, STALE, WIDTH), BF16),
            pltpu.VMEM((GROUPS - 1, 2, TILE, WIDTH), BF16),
            pltpu.VMEM((2, ROWS, WIDTH), BF16),
            pltpu.VMEM((ROWS, WIDTH), BF16),
            pltpu.VMEM((RING, TILE, TILE), F32),
            pltpu.VMEM((BLOCK, KEYS), F32),
            pltpu.VMEM((OWN_HEADS, RING, 8, TILE), F32),
            pltpu.VMEM((OWN_HEADS, RING, 8, TILE), F32),
            dma((OWN_HEADS, RING, 2)), dma((OWN_HEADS, RING, 2)),
            dma((OWN_HEADS, RING)), dma((OWN_HEADS, RING)),
            dma((OWN_HEADS, 2)), dma((OWN_HEADS, 2)),
            dma((OWN_HEADS, RING)), dma((OWN_HEADS, RING)),
            dma((OWN_HEADS, RING)), dma((OWN_HEADS, RING)),
            dma((RING,)), dma((RING,)),
            dma((GROUPS,)), dma((GROUPS,)),
            dma((3,)),
        ],
        compiler_params=pltpu.CompilerParams(
            collective_id=0, has_side_effects=True, vmem_limit_bytes=58 * 2**20
        ),
        cost_estimate=pl.CostEstimate(
            flops=4 * ROWS * HEAD_DIM * HEADS * (KEYS + STALE),
            bytes_accessed=8 * ROWS * WIDTH * 2,
            transcendentals=ROWS * HEADS * (KEYS + STALE),
        ),
    )(queries, keys, values, stale_keys, stale_values, tile_mask, stale_pick)


def solution(mesh):
    wide = P(("tm", "seq"), None)
    placed = (wide, wide, wide, wide, wide, P(("tm", "seq"), None, None), wide)
    return jax.shard_map(body, mesh=mesh, in_specs=placed, out_specs=wide, check_vma=False)
```

time: 984 us -> 279 us (0.28)
  the two profiles are of different devices: /device:TPU:34 before, /device:TPU:1 now
where the time goes in v1:
time: 279 us; the launch traced here: 278 us
  Pallas kernels  273 us (98%)
  local copies, waits for them, and re-layouts  5.16 us (2%)
    pallas_call x1, Pallas kernels, body(): pl.pallas_call(kernel, out_shape=jax.ShapeDtypeStruct((ROWS, WIDTH), BF16...  273 us

profile of v1, /device:TPU:1, one launch (start us, length us, event | category | flops | bytes accessed | tf_op | source)
XLA Modules:
  0.0 278.4 jit_solution(15096569693470166280)
XLA Ops:
  0.0 1.4 copy.8.mask_ref
  1.4 273.2 %shard_map.73 = bf16[512,3072]{1,0:T(8,128)(2,1)} custom-call(bf16[512,3072]{1,0:T(8,128)(2,1)} %q_hbm.1, bf16[512,3072]{1,0:T(8,128)(2,1)} %k_hbm.1, bf16[512,3072]{1,0:T(8,128)(2,1)} %v_hbm.1, bf16[512,3072]{1,0:T(8,128)(2,1)} %sk_hbm.1, bf16[512,3072]{1,0:T(8,128)(2,1)} %sv_hbm.1, s32[4,7,4]{2,1,0:T(8,128)} %copy.8.mask_ref, s32[1,4]{1,0:T(1,128)} %pick_ref.1), custom_call_target="tpu_custom_call" | custom-call | flops 25769803776 | bytes 25165824 | tf_op jit(solution)/shard_map/pallas_call | solution.py:361
  274.6 3.8 %copy.10 = bf16[512,3072]{1,0:T(8,128)(2,1)} copy(bf16[512,3072]{1,0:T(8,128)(2,1)} %shard_map.73) | data formatting | bytes 6291456

commit v2 on v1

--- a/solution.py
+++ b/solution.py
@@ -18,12 +18,16 @@
 WIDTH = HEADS * HEAD_DIM
 GROUPS = 4
 SHARDS = 32
+RUNS = 8
+LATE = 4
+MIDDLE = RUNS // 2
 RING = 4
 OWN_HEADS = HEADS // RING
 SLOTS = RING + 2 * REACH
 KEYS = WINDOW * ROWS
 STALE = GROUPS * TILE
 BLOCK = 256
+HALF = REACH * ROWS // 2
 FACTOR = math.log2(math.e) / math.sqrt(HEAD_DIM)
 LOW = -1e30
 MESH = pl.DeviceIdType.MESH
@@ -32,21 +36,34 @@
 
 
 def scores(q, k):
-    return lax.dot_general(q, k, (((1,), (1,)), ((), ())), preferred_element_type=F32) * FACTOR
+    return lax.dot_general(q, k, (((1,), (1,)), ((), ())), preferred_element_type=F32)
+
+
+def with_sums(p, v):
+    ones = jnp.ones((v.shape[0], HEAD_DIM), BF16)
+    return jnp.dot(p, jnp.concatenate([v, ones], axis=1), preferred_element_type=F32)
 
 
 def kernel(
     q_hbm, k_hbm, v_hbm, sk_hbm, sv_hbm, mask_ref, pick_ref, out_ref,
-    kv, qr, ob, oh, stale, stale_out, staging, qh, allow, sc, lse_out, lse_in,
-    kv_ss, kv_rs, q_ss, q_rs, halo_ss, halo_rs, o_ss, o_rs, l_ss, l_rs,
+    kv, qr, ob, oh, stale, stale_out, staging, qh, allow, sc_a, sc_b, top_a, top_b, lse_out, lse_in,
+    kv_ss, kv_rs, q_ss, q_rs, halo_ss, halo_rs, relay_rs, pass_ss, o_ss, o_rs, l_ss, l_rs,
     a_ss, a_rs, st_ss, st_rs, loc,
 ):
     tm = lax.axis_index("tm")
     s = lax.axis_index("seq")
     z = lax.rem(s, RING)
     row0 = s - z
+    run = s // RING
     has_low = s >= RING
     has_high = s < SHARDS - RING
+    mid_low = run == MIDDLE - 1
+    mid_high = run == MIDDLE
+    first_run = run == 0
+    last_run = run == RUNS - 1
+    corner = first_run | mid_low | mid_high | last_run
+    near = jnp.where(run < MIDDLE, s + MIDDLE * RING, s - MIDDLE * RING)
+    far = jnp.where(first_run | mid_high, s + (MIDDLE - 1) * RING, s - (MIDDLE - 1) * RING)
 
     def ring(d):
         return (tm, row0 + lax.rem(z + d, RING))
@@ -67,6 +84,11 @@
     @pl.when(has_high)
     def _():
         pl.semaphore_signal(bar, inc=1, device_id=(tm, s + RING), device_id_type=MESH)
+
+    @pl.when(corner)
+    def _():
+        pl.semaphore_signal(bar, inc=1, device_id=(tm, near), device_id_type=MESH)
+        pl.semaphore_signal(bar, inc=1, device_id=(tm, far), device_id_type=MESH)
 
     pltpu.make_async_copy(q_hbm, qh, loc.at[0]).start()
     pltpu.make_async_copy(sk_hbm, staging.at[0], loc.at[1]).start()
@@ -83,7 +105,9 @@
                 allow[z, pl.ds(t * 32 + o * TILES_DEV + j, 1), :] = value
 
     pl.semaphore_wait(
-        bar, RING - 1 + GROUPS - 1 + has_low.astype(jnp.int32) + has_high.astype(jnp.int32)
+        bar,
+        RING - 1 + GROUPS - 1 + has_low.astype(jnp.int32) + has_high.astype(jnp.int32)
+        + 2 * corner.astype(jnp.int32),
     )
 
     def kv_copy(i, d, which):
@@ -113,18 +137,41 @@
             allow.at[z], allow.at[z], a_ss.at[d], a_rs.at[d],
             device_id=ring(d), device_id_type=MESH)
 
-    def halo_copy(i, up):
-        if up:
-            src = kv.at[i, :, pl.ds((RING) * ROWS, REACH * ROWS), :]
-            dst = kv.at[i, :, pl.ds(0, REACH * ROWS), :]
-            dev = (tm, s + RING)
-        else:
-            src = kv.at[i, :, pl.ds(REACH * ROWS, REACH * ROWS), :]
-            dst = kv.at[i, :, pl.ds((RING + REACH) * ROWS, REACH * ROWS), :]
-            dev = (tm, s - RING)
+    LOW_SLOTS, OWN_LOW, OWN_HIGH, HIGH_SLOTS = 0, REACH * ROWS, RING * ROWS, (RING + REACH) * ROWS
+
+    def halo_copy(i, up, half):
+        start, land = (OWN_HIGH, LOW_SLOTS) if up else (OWN_LOW, HIGH_SLOTS)
         n = 0 if up else 1
         return pltpu.make_async_remote_copy(
-            src, dst, halo_ss.at[i, n], halo_rs.at[i, n], device_id=dev, device_id_type=MESH)
+            kv.at[i, :, pl.ds(start + half * HALF, HALF), :],
+            kv.at[i, :, pl.ds(land + half * HALF, HALF), :],
+            halo_ss.at[i, n, half], halo_rs.at[i, n, half],
+            device_id=(tm, s + RING if up else s - RING), device_id_type=MESH)
+
+    def relay_copy(i, up):
+        start, land = (OWN_HIGH, HIGH_SLOTS) if up else (OWN_LOW, LOW_SLOTS)
+        n = 0 if up else 1
+        return pltpu.make_async_remote_copy(
+            kv.at[i, :, pl.ds(start + HALF, HALF), :], kv.at[i, :, pl.ds(land, HALF), :],
+            halo_ss.at[i, n, 1], relay_rs.at[i], device_id=(tm, near), device_id_type=MESH)
+
+    def pass_copy(i, up):
+        start, land = (HIGH_SLOTS, LOW_SLOTS) if up else (LOW_SLOTS, HIGH_SLOTS)
+        n = 0 if up else 1
+        return pltpu.make_async_remote_copy(
+            kv.at[i, :, pl.ds(start, HALF), :], kv.at[i, :, pl.ds(land + HALF, HALF), :],
+            pass_ss.at[i], halo_rs.at[i, n, 1], device_id=(tm, far), device_id_type=MESH)
+
+    def hand_on(i):
+        @pl.when(last_run)
+        def _():
+            relay_copy(i, True).wait_recv()
+            pass_copy(i, True).start()
+
+        @pl.when(first_run)
+        def _():
+            relay_copy(i, False).wait_recv()
+            pass_copy(i, False).start()
 
     def o_copy(i, d):
         j = lax.rem(z + d, RING)
@@ -162,32 +209,49 @@
 
         @pl.when(has_high)
         def _():
-            halo_copy(i, True).start()
+            halo_copy(i, True, 0).start()
 
         @pl.when(has_low)
         def _():
-            halo_copy(i, False).start()
+            halo_copy(i, False, 0).start()
+
+        @pl.when(has_high & jnp.logical_not(mid_low))
+        def _():
+            halo_copy(i, True, 1).start()
+
+        @pl.when(has_low & jnp.logical_not(mid_high))
+        def _():
+            halo_copy(i, False, 1).start()
+
+        @pl.when(mid_low)
+        def _():
+            relay_copy(i, True).start()
+
+        @pl.when(mid_high)
+        def _():
+            relay_copy(i, False).start()
 
     for d in range(1, RING):
         allow_copy(d).start()
-    start_kv(0)
-    start_kv(1)
-    start_q(0)
+    @pl.loop(0, OWN_HEADS)
+    def _(i):
+        start_kv(i)
+        start_q(i)
 
     @pl.when(jnp.logical_not(has_low))
     def _():
         @pl.loop(0, OWN_HEADS)
         def _(i):
             for which in range(2):
-                kv[i, which, pl.ds(0, REACH * ROWS), :] = jnp.zeros((REACH * ROWS, HEAD_DIM), BF16)
+                kv[i, which, pl.ds(HALF, HALF), :] = jnp.zeros((HALF, HEAD_DIM), BF16)
 
     @pl.when(jnp.logical_not(has_high))
     def _():
         @pl.loop(0, OWN_HEADS)
         def _(i):
             for which in range(2):
-                kv[i, which, pl.ds((RING + REACH) * ROWS, REACH * ROWS), :] = jnp.zeros(
-                    (REACH * ROWS, HEAD_DIM), BF16)
+                kv[i, which, pl.ds((RING + REACH) * ROWS + HALF, HALF), :] = jnp.zeros(
+                    (HALF, HEAD_DIM), BF16)
 
     pltpu.make_async_copy(sk_hbm, staging.at[0], loc.at[1]).wait()
     pltpu.make_async_copy(sv_hbm, staging.at[1], loc.at[2]).wait()
@@ -215,51 +279,68 @@
         allow_copy(d).wait_recv()
     pltpu.make_async_copy(q_hbm, qh, loc.at[0]).wait()
 
-    def fresh(i):
-        @pl.loop(0, RING * ROWS // BLOCK)
-        def _(n):
-            j = n // (ROWS // BLOCK)
-            b = n % (ROWS // BLOCK)
-            q = qr[i, pl.ds(pl.multiple_of(n * BLOCK, BLOCK), BLOCK), :]
-            base = j * ROWS
-            mx = None
-            for c in range(WINDOW):
-                k = kv[i, 0, pl.ds(pl.multiple_of(base + c * ROWS, ROWS), ROWS), :]
-                x = scores(q, k)
+    PARTS = ROWS // BLOCK
+
+    def both(i, scored, weighed):
+        top = acc = None
+        if scored is not None:
+            h, b, s_ref, top_ref = scored
+            j = lax.rem(z + 1 + h, RING)
+            q = qr[i, pl.ds(pl.multiple_of(j * ROWS + b * BLOCK, BLOCK), BLOCK), :]
+            base = pl.multiple_of(j * ROWS, ROWS)
+        if weighed is not None:
+            h2, b2, p_ref, ptop_ref = weighed
+            j2 = lax.rem(z + 1 + h2, RING)
+            base2 = pl.multiple_of(j2 * ROWS, ROWS)
+            shift = ptop_ref[...]
+            acc = jnp.zeros((BLOCK, 2 * HEAD_DIM), F32)
+        for c in range(WINDOW):
+            if scored is not None:
+                x = scores(q, kv[i, 0, pl.ds(pl.multiple_of(base + c * ROWS, ROWS), ROWS), :])
                 parts = []
                 for tt in range(BLOCK // TILE):
-                    t = b * (BLOCK // TILE) + tt
-                    row = []
+                    most = None
                     for kk in range(TILES_DEV):
-                        a = allow[j, pl.ds(t * 32 + c * TILES_DEV + kk, 1), :]
+                        pair = (b * (BLOCK // TILE) + tt) * 32 + c * TILES_DEV + kk
                         y = x[tt * TILE:(tt + 1) * TILE, kk * TILE:(kk + 1) * TILE]
-                        y = jnp.where(a > 0, y, LOW)
-                        sc[tt * TILE:(tt + 1) * TILE, pl.ds(c * ROWS + kk * TILE, TILE)] = y
-                        row.append(y)
-                    parts.append(jnp.maximum(jnp.maximum(row[0], row[1]), jnp.maximum(row[2], row[3])))
+                        y = jnp.where(allow[j, pl.ds(pair, 1), :] > 0, y, LOW)
+                        s_ref[tt * TILE:(tt + 1) * TILE, pl.ds(c * ROWS + kk * TILE, TILE)] = y
+                        most = y if most is None else jnp.maximum(most, y)
+                    parts.append(most)
                 x = jnp.concatenate(parts, axis=0)
-                mx = x if mx is None else jnp.maximum(mx, x)
-            m = jnp.max(mx, axis=1, keepdims=True)
-            total = jnp.zeros((BLOCK, TILE), F32)
-            acc = jnp.zeros((BLOCK, HEAD_DIM), F32)
-            for c in range(WINDOW):
-                p = jnp.exp2(sc[:, pl.ds(c * ROWS, ROWS)] - m)
-                for kk in range(TILES_DEV):
-                    total += p[:, kk * TILE:(kk + 1) * TILE]
-                v = kv[i, 1, pl.ds(pl.multiple_of(base + c * ROWS, ROWS), ROWS), :]
-                acc += jnp.dot(p.astype(BF16), v, preferred_element_type=F32)
-            total = jnp.sum(total, axis=1, keepdims=True)
-            o = (acc / total).astype(BF16)
-            ob[i, pl.ds(pl.multiple_of(n * BLOCK, BLOCK), BLOCK), :] = o
-            lse = jnp.broadcast_to(m + jnp.log2(total), (BLOCK, TILE))
+                top = x if top is None else jnp.maximum(top, x)
+            if weighed is not None:
+                p = [
+                    jnp.exp2(p_ref[:, pl.ds(c * ROWS + kk * TILE, TILE)] * FACTOR - shift).astype(BF16)
+                    for kk in range(TILES_DEV)
+                ]
+                v = kv[i, 1, pl.ds(pl.multiple_of(base2 + c * ROWS, ROWS), ROWS), :]
+                acc += with_sums(jnp.concatenate(p, axis=1), v)
+        if scored is not None:
+            top_ref[...] = jnp.broadcast_to(
+                jnp.max(top, axis=1, keepdims=True) * FACTOR, (BLOCK, TILE))
+        if weighed is not None:
+            total = acc[:, HEAD_DIM:]
+            ob[i, pl.ds(pl.multiple_of(j2 * ROWS + b2 * BLOCK, BLOCK), BLOCK), :] = (
+                acc[:, :HEAD_DIM] / total).astype(BF16)
+            lse = shift + jnp.log2(total)
             for tt in range(BLOCK // TILE):
                 turned = lse[tt * TILE:(tt + 1) * TILE, :].T
-                lse_out[i, j, pl.ds(b * (BLOCK // TILE) + tt, 1), :] = turned[0:1, :]
-
-    def send_home(i):
-        for d in range(1, RING):
-            o_copy(i, d).start()
-            l_copy(i, d).start()
+                lse_out[i, j2, pl.ds(b2 * (BLOCK // TILE) + tt, 1), :] = turned[0:1, :]
+
+    def fresh(i):
+        a, b = (sc_a, top_a), (sc_b, top_b)
+        both(i, (0, 0, *a), None)
+
+        @pl.loop(0, RING - 1)
+        def _(h):
+            both(i, (h, 1, *b), (h, 0, *a))
+            both(i, (h + 1, 0, *a), (h, 1, *b))
+            o_copy(i, h + 1).start()
+            l_copy(i, h + 1).start()
+
+        both(i, (RING - 1, 1, *b), (RING - 1, 0, *a))
+        both(i, None, (RING - 1, 1, *b))
         oh[i, z] = ob[i, pl.ds(pl.multiple_of(z * ROWS, ROWS), ROWS), :]
         lse_in[i, z] = lse_out[i, z]
 
@@ -275,7 +356,7 @@
             head = owner * OWN_HEADS + i
             cols = pl.ds(pl.multiple_of(head * HEAD_DIM, HEAD_DIM), HEAD_DIM)
             rows = pl.ds(pl.multiple_of(b * BLOCK, BLOCK), BLOCK)
-            x = scores(qh[rows, cols], stale[0, :, cols])
+            x = scores(qh[rows, cols], stale[0, :, cols]) * FACTOR
             lse = []
             for tt in range(BLOCK // TILE):
                 one = lse_in[i, owner, pl.ds(b * (BLOCK // TILE) + tt, 1), :]
@@ -284,31 +365,33 @@
             m = jnp.maximum(jnp.max(x, axis=1, keepdims=True), lse)
             old = jnp.exp2(lse - m)
             p = [jnp.exp2(x[:, k * TILE:(k + 1) * TILE] - m) for k in range(GROUPS)]
-            total = old + jnp.sum(p[0] + p[1] + p[2] + p[3], axis=1, keepdims=True)
-            acc = jnp.dot(jnp.concatenate(p, axis=1).astype(BF16), stale[1, :, cols],
-                          preferred_element_type=F32)
+            acc = with_sums(jnp.concatenate(p, axis=1).astype(BF16), stale[1, :, cols])
             o = oh[i, owner, rows, :].astype(F32)
-            out_ref[rows, cols] = ((old * o + acc) / total).astype(BF16)
+            out_ref[rows, cols] = (
+                (old * o + acc[:, :HEAD_DIM]) / (old + acc[:, HEAD_DIM:])).astype(BF16)
 
     @pl.loop(0, OWN_HEADS)
     def _(i):
         @pl.when(i < OWN_HEADS - 2)
         def _():
-            start_kv(i + 2)
+            pass
 
         @pl.when(i < OWN_HEADS - 1)
         def _():
-            start_q(i + 1)
             halo(i + 1)
 
-        @pl.when(i == 2)
+        hand_on(i)
+
+        @pl.when(i == LATE)
         def _():
             for d in range(1, GROUPS):
                 stale_copy(d).wait_recv()
 
-        @pl.when(i >= 2)
-        def _():
-            merge(i - 2)
+        @pl.when(i >= LATE)
+        def _():
+            @pl.loop(2 * (i - LATE), 2 * (i - LATE) + 2)
+            def _(n):
+                merge(n)
 
         for d in range(RING):
             if d == 0:
@@ -318,16 +401,17 @@
 
         @pl.when(has_low)
         def _():
-            halo_copy(i, True).wait_recv()
+            halo_copy(i, True, 0).wait_recv()
+            halo_copy(i, True, 1).wait_recv()
 
         @pl.when(has_high)
         def _():
-            halo_copy(i, False).wait_recv()
+            halo_copy(i, False, 0).wait_recv()
+            halo_copy(i, False, 1).wait_recv()
 
         fresh(i)
-        send_home(i)
-
-    @pl.loop(OWN_HEADS - 2, OWN_HEADS)
+
+    @pl.loop(2 * (OWN_HEADS - LATE), OWN_HEADS)
     def _(i):
         merge(i)
 
@@ -347,11 +431,17 @@
 
         @pl.when(has_high)
         def _():
-            halo_copy(i, True).wait_send()
+            halo_copy(i, True, 0).wait_send()
+            halo_copy(i, True, 1).wait_send()
 
         @pl.when(has_low)
         def _():
-            halo_copy(i, False).wait_send()
+            halo_copy(i, False, 0).wait_send()
+            halo_copy(i, False, 1).wait_send()
+
+        @pl.when(last_run | first_run)
+        def _():
+            pass_copy(i, True).wait_send()
 
 
 def body(queries, keys, values, stale_keys, stale_values, tile_mask, stale_pick):
@@ -373,12 +463,14 @@
             pltpu.VMEM((2, ROWS, WIDTH), BF16),
             pltpu.VMEM((ROWS, WIDTH), BF16),
             pltpu.VMEM((RING, TILE, TILE), F32),
-            pltpu.VMEM((BLOCK, KEYS), F32),
+            pltpu.VMEM((BLOCK, KEYS), F32), pltpu.VMEM((BLOCK, KEYS), F32),
+            pltpu.VMEM((BLOCK, TILE), F32), pltpu.VMEM((BLOCK, TILE), F32),
             pltpu.VMEM((OWN_HEADS, RING, 8, TILE), F32),
             pltpu.VMEM((OWN_HEADS, RING, 8, TILE), F32),
             dma((OWN_HEADS, RING, 2)), dma((OWN_HEADS, RING, 2)),
             dma((OWN_HEADS, RING)), dma((OWN_HEADS, RING)),
-            dma((OWN_HEADS, 2)), dma((OWN_HEADS, 2)),
+            dma((OWN_HEADS, 2, 2)), dma((OWN_HEADS, 2, 2)),
+            dma((OWN_HEADS,)), dma((OWN_HEADS,)),
             dma((OWN_HEADS, RING)), dma((OWN_HEADS, RING)),
             dma((OWN_HEADS, RING)), dma((OWN_HEADS, RING)),
             dma((RING,)), dma((RING,)),

time: 279 us -> 211 us (0.76)
  the two profiles are of different devices: /device:TPU:1 before, /device:TPU:26 now
where the time goes in v2:
time: 211 us; the launch traced here: 210 us
  Pallas kernels  205 us (97%)
  local copies, waits for them, and re-layouts  5.16 us (2%)
    pallas_call x1, Pallas kernels, body(): pl.pallas_call(kernel, out_shape=jax.ShapeDtypeStruct((ROWS, WIDTH), BF16...  205 us
    unnamed x2, local copies, waits for them, and re-layouts  5.16 us

profile of v2, /device:TPU:26, one launch (start us, length us, event | category | flops | bytes accessed | tf_op | source)
XLA Modules:
  0.0 210.3 jit_solution(5407528554756302526)
XLA Ops:
  0.0 1.4 copy.8.mask_ref
  1.4 205.1 %shard_map.73 = bf16[512,3072]{1,0:T(8,128)(2,1)} custom-call(bf16[512,3072]{1,0:T(8,128)(2,1)} %q_hbm.1, bf16[512,3072]{1,0:T(8,128)(2,1)} %k_hbm.1, bf16[512,3072]{1,0:T(8,128)(2,1)} %v_hbm.1, bf16[512,3072]{1,0:T(8,128)(2,1)} %sk_hbm.1, bf16[512,3072]{1,0:T(8,128)(2,1)} %sv_hbm.1, s32[4,7,4]{2,1,0:T(8,128)} %copy.8.mask_ref, s32[1,4]{1,0:T(1,128)} %pick_ref.1), custom_call_target="tpu_custom_call" | custom-call | flops 25769803776 | bytes 25165824 | tf_op jit(solution)/shard_map/pallas_call | solution.py:451
  206.6 3.8 %copy.10 = bf16[512,3072]{1,0:T(8,128)(2,1)} copy(bf16[512,3072]{1,0:T(8,128)(2,1)} %shard_map.73) | data formatting | bytes 6291456

commit v3 on v2

--- a/solution.py
+++ b/solution.py
@@ -19,7 +19,7 @@
 GROUPS = 4
 SHARDS = 32
 RUNS = 8
-LATE = 4
+EARLY = 2
 MIDDLE = RUNS // 2
 RING = 4
 OWN_HEADS = HEADS // RING
@@ -90,20 +90,6 @@
         pl.semaphore_signal(bar, inc=1, device_id=(tm, near), device_id_type=MESH)
         pl.semaphore_signal(bar, inc=1, device_id=(tm, far), device_id_type=MESH)
 
-    pltpu.make_async_copy(q_hbm, qh, loc.at[0]).start()
-    pltpu.make_async_copy(sk_hbm, staging.at[0], loc.at[1]).start()
-    pltpu.make_async_copy(sv_hbm, staging.at[1], loc.at[2]).start()
-
-    for t in range(TILES_DEV):
-        for o in range(WINDOW):
-            there = ((s + (o - REACH) >= 0) & (s + (o - REACH) < SHARDS)).astype(F32)
-            for j in range(TILES_DEV):
-                if o == REACH and j == t:
-                    value = jnp.ones((1, TILE), F32)
-                else:
-                    value = jnp.full((1, TILE), mask_ref[t, o, j], jnp.int32).astype(F32) * there
-                allow[z, pl.ds(t * 32 + o * TILES_DEV + j, 1), :] = value
-
     pl.semaphore_wait(
         bar,
         RING - 1 + GROUPS - 1 + has_low.astype(jnp.int32) + has_high.astype(jnp.int32)
@@ -185,10 +171,14 @@
             lse_out.at[i, j], lse_in.at[i, z],
             l_ss.at[i, d], l_rs.at[i, d], device_id=ring(d), device_id_type=MESH)
 
-    def stale_copy(d):
-        return pltpu.make_async_remote_copy(
-            stale_out.at[d - 1], stale.at[:, pl.ds(pl.multiple_of(tm * TILE, TILE), TILE), :],
-            st_ss.at[d], st_rs.at[d], device_id=group(d), device_id_type=MESH)
+    def stale_copy(i, d):
+        return pltpu.make_async_remote_copy(
+            stale_out.at[i, d - 1], stale.at[i, :, pl.ds(pl.multiple_of(tm * TILE, TILE), TILE), :],
+            st_ss.at[i, d], st_rs.at[i, d], device_id=group(d), device_id_type=MESH)
+
+    def start_stale(i):
+        for d in (2, 1, 3):
+            stale_copy(i, d).start()
 
     def start_kv(i):
         for d in (2, 1, 3, 0):
@@ -231,9 +221,25 @@
         def _():
             relay_copy(i, False).start()
 
+    start_kv(0)
+    start_q(0)
+    pltpu.make_async_copy(q_hbm, qh, loc.at[0]).start()
+    pltpu.make_async_copy(sk_hbm, staging.at[0], loc.at[1]).start()
+    pltpu.make_async_copy(sv_hbm, staging.at[1], loc.at[2]).start()
+
+    for t in range(TILES_DEV):
+        for o in range(WINDOW):
+            there = ((s + (o - REACH) >= 0) & (s + (o - REACH) < SHARDS)).astype(F32)
+            for j in range(TILES_DEV):
+                if o == REACH and j == t:
+                    value = jnp.ones((1, TILE), F32)
+                else:
+                    value = jnp.full((1, TILE), mask_ref[t, j, o], jnp.int32).astype(F32) * there
+                allow[z, pl.ds(t * 32 + o * TILES_DEV + j, 1), :] = value
     for d in range(1, RING):
         allow_copy(d).start()
-    @pl.loop(0, OWN_HEADS)
+
+    @pl.loop(1, OWN_HEADS)
     def _(i):
         start_kv(i)
         start_q(i)
@@ -262,24 +268,23 @@
             for t in range(TILES_DEV)
         ]
         for which in range(2):
-            @pl.loop(0, HEADS)
-            def _(h, d=d, which=which, chosen=chosen):
-                cols = pl.ds(pl.multiple_of(h * HEAD_DIM, HEAD_DIM), HEAD_DIM)
-                one = [staging[which, pl.ds(t * TILE, TILE), cols] * chosen[t] for t in range(TILES_DEV)]
-                one = (one[0] + one[1]) + (one[2] + one[3])
-                if d == 0:
-                    stale[which, pl.ds(pl.multiple_of(tm * TILE, TILE), TILE), cols] = one
-                else:
-                    stale_out[d - 1, which, :, cols] = one
-        if d:
-            stale_copy(d).start()
+            @pl.loop(0, OWN_HEADS)
+            def _(i, d=d, which=which, chosen=chosen):
+                for owner in range(RING):
+                    cols = pl.ds(pl.multiple_of((owner * OWN_HEADS + i) * HEAD_DIM, HEAD_DIM), HEAD_DIM)
+                    one = [staging[which, pl.ds(t * TILE, TILE), cols] * chosen[t] for t in range(TILES_DEV)]
+                    one = (one[0] + one[1]) + (one[2] + one[3])
+                    place = slice(owner * HEAD_DIM, (owner + 1) * HEAD_DIM)
+                    if d == 0:
+                        stale[i, which, pl.ds(pl.multiple_of(tm * TILE, TILE), TILE), place] = one
+                    else:
+                        stale_out[i, d - 1, which, :, place] = one
 
     halo(0)
+    start_stale(0)
     for d in range(1, RING):
         allow_copy(d).wait_recv()
     pltpu.make_async_copy(q_hbm, qh, loc.at[0]).wait()
-
-    PARTS = ROWS // BLOCK
 
     def both(i, scored, weighed):
         top = acc = None
@@ -348,6 +353,7 @@
         for d in range(1, RING):
             o_copy(i, d).wait_recv()
             l_copy(i, d).wait_recv()
+            stale_copy(i, d).wait_recv()
 
         @pl.loop(0, RING * ROWS // BLOCK)
         def _(n):
@@ -356,7 +362,8 @@
             head = owner * OWN_HEADS + i
             cols = pl.ds(pl.multiple_of(head * HEAD_DIM, HEAD_DIM), HEAD_DIM)
             rows = pl.ds(pl.multiple_of(b * BLOCK, BLOCK), BLOCK)
-            x = scores(qh[rows, cols], stale[0, :, cols]) * FACTOR
+            place = pl.ds(pl.multiple_of(owner * HEAD_DIM, HEAD_DIM), HEAD_DIM)
+            x = scores(qh[rows, cols], stale[i, 0, :, place]) * FACTOR
             lse = []
             for tt in range(BLOCK // TILE):
                 one = lse_in[i, owner, pl.ds(b * (BLOCK // TILE) + tt, 1), :]
@@ -365,7 +372,7 @@
             m = jnp.maximum(jnp.max(x, axis=1, keepdims=True), lse)
             old = jnp.exp2(lse - m)
             p = [jnp.exp2(x[:, k * TILE:(k + 1) * TILE] - m) for k in range(GROUPS)]
-            acc = with_sums(jnp.concatenate(p, axis=1).astype(BF16), stale[1, :, cols])
+            acc = with_sums(jnp.concatenate(p, axis=1).astype(BF16), stale[i, 1, :, place])
             o = oh[i, owner, rows, :].astype(F32)
             out_ref[rows, cols] = (
                 (old * o + acc[:, :HEAD_DIM]) / (old + acc[:, HEAD_DIM:])).astype(BF16)
@@ -379,17 +386,15 @@
         @pl.when(i < OWN_HEADS - 1)
         def _():
             halo(i + 1)
-
-        hand_on(i)
-
-        @pl.when(i == LATE)
-        def _():
-            for d in range(1, GROUPS):
-                stale_copy(d).wait_recv()
-
-        @pl.when(i >= LATE)
-        def _():
-            @pl.loop(2 * (i - LATE), 2 * (i - LATE) + 2)
+            start_stale(i + 1)
+
+        @pl.when(i == 0)
+        def _():
+            hand_on(0)
+
+        @pl.when(i == OWN_HEADS - 1)
+        def _():
+            @pl.loop(0, EARLY)
             def _(n):
                 merge(n)
 
@@ -411,14 +416,16 @@
 
         fresh(i)
 
-    @pl.loop(2 * (OWN_HEADS - LATE), OWN_HEADS)
+        @pl.when(i < OWN_HEADS - 1)
+        def _():
+            hand_on(i + 1)
+
+    @pl.loop(EARLY, OWN_HEADS)
     def _(i):
         merge(i)
 
     for d in range(1, RING):
         allow_copy(d).wait_send()
-    for d in range(1, GROUPS):
-        stale_copy(d).wait_send()
 
     @pl.loop(0, OWN_HEADS)
     def _(i):
@@ -428,6 +435,7 @@
             q_copy(i, d).wait_send()
             o_copy(i, d).wait_send()
             l_copy(i, d).wait_send()
+            stale_copy(i, d).wait_send()
 
         @pl.when(has_high)
         def _():
@@ -458,8 +466,8 @@
             pltpu.VMEM((OWN_HEADS, RING * ROWS, HEAD_DIM), BF16),
             pltpu.VMEM((OWN_HEADS, RING * ROWS, HEAD_DIM), BF16),
             pltpu.VMEM((OWN_HEADS, RING, ROWS, HEAD_DIM), BF16),
-            pltpu.VMEM((2, STALE, WIDTH), BF16),
-            pltpu.VMEM((GROUPS - 1, 2, TILE, WIDTH), BF16),
+            pltpu.VMEM((OWN_HEADS, 2, STALE, RING * HEAD_DIM), BF16),
+            pltpu.VMEM((OWN_HEADS, GROUPS - 1, 2, TILE, RING * HEAD_DIM), BF16),
             pltpu.VMEM((2, ROWS, WIDTH), BF16),
             pltpu.VMEM((ROWS, WIDTH), BF16),
             pltpu.VMEM((RING, TILE, TILE), F32),
@@ -474,7 +482,7 @@
             dma((OWN_HEADS, RING)), dma((OWN_HEADS, RING)),
             dma((OWN_HEADS, RING)), dma((OWN_HEADS, RING)),
             dma((RING,)), dma((RING,)),
-            dma((GROUPS,)), dma((GROUPS,)),
+            dma((OWN_HEADS, GROUPS)), dma((OWN_HEADS, GROUPS)),
             dma((3,)),
         ],
         compiler_params=pltpu.CompilerParams(
@@ -485,7 +493,7 @@
             bytes_accessed=8 * ROWS * WIDTH * 2,
             transcendentals=ROWS * HEADS * (KEYS + STALE),
         ),
-    )(queries, keys, values, stale_keys, stale_values, tile_mask, stale_pick)
+    )(queries, keys, values, stale_keys, stale_values, tile_mask.transpose(0, 2, 1), stale_pick)
 
 
 def solution(mesh):

time: 211 us -> 181 us (0.86)
  the two profiles are of different devices: /device:TPU:26 before, /device:TPU:1 now
where the time goes in v3:
time: 181 us; the launch traced here: 179 us
  Pallas kernels  175 us (97%)
  local copies, waits for them, and re-layouts  3.76 us (2%)
    pallas_call x1, Pallas kernels, body(): pl.pallas_call(kernel, out_shape=jax.ShapeDtypeStruct((ROWS, WIDTH), BF16...  175 us
    unnamed x1, local copies, waits for them, and re-layouts  3.76 us

profile of v3, /device:TPU:1, one launch (start us, length us, event | category | flops | bytes accessed | tf_op | source)
XLA Modules:
  0.0 178.9 jit_solution(15488539375940235206)
XLA Ops:
  0.0 175.1 %shard_map.73 = bf16[512,3072]{1,0:T(8,128)(2,1)} custom-call(bf16[512,3072]{1,0:T(8,128)(2,1)} %q_hbm.1, bf16[512,3072]{1,0:T(8,128)(2,1)} %k_hbm.1, bf16[512,3072]{1,0:T(8,128)(2,1)} %v_hbm.1, bf16[512,3072]{1,0:T(8,128)(2,1)} %sk_hbm.1, bf16[512,3072]{1,0:T(8,128)(2,1)} %sv_hbm.1, s32[4,4,7]{2,1,0:T(4,128)} %bitcast.1, s32[1,4]{1,0:T(1,128)} %pick_ref.1), custom_call_target="tpu_custom_call" | custom-call | flops 25769803776 | bytes 25165824 | tf_op jit(solution)/shard_map/pallas_call | solution.py:459
  175.1 3.8 %copy.9 = bf16[512,3072]{1,0:T(8,128)(2,1)} copy(bf16[512,3072]{1,0:T(8,128)(2,1)} %shard_map.73) | data formatting | bytes 6291456

commit v4 on v3

--- a/solution.py
+++ b/solution.py
@@ -45,10 +45,10 @@
 
 
 def kernel(
-    q_hbm, k_hbm, v_hbm, sk_hbm, sv_hbm, mask_ref, pick_ref, out_ref,
-    kv, qr, ob, oh, stale, stale_out, staging, qh, allow, sc_a, sc_b, top_a, top_b, lse_out, lse_in,
+    q_hbm, k_hbm, v_hbm, sk_hbm, sv_hbm, mask_ref, pick_ref, out_hbm,
+    kv, qr, ob, oh, stale, stale_out, staging, qh, allow, sc_a, sc_b, top_a, top_b, lse_out, lse_in, lse_st, merged,
     kv_ss, kv_rs, q_ss, q_rs, halo_ss, halo_rs, relay_rs, pass_ss, o_ss, o_rs, l_ss, l_rs,
-    a_ss, a_rs, st_ss, st_rs, loc,
+    a_ss, a_rs, st_ss, st_rs, loc, out_sem,
 ):
     tm = lax.axis_index("tm")
     s = lax.axis_index("seq")
@@ -125,39 +125,38 @@
 
     LOW_SLOTS, OWN_LOW, OWN_HIGH, HIGH_SLOTS = 0, REACH * ROWS, RING * ROWS, (RING + REACH) * ROWS
 
-    def halo_copy(i, up, half):
+    def halo_copy(i, up, half, which):
         start, land = (OWN_HIGH, LOW_SLOTS) if up else (OWN_LOW, HIGH_SLOTS)
         n = 0 if up else 1
         return pltpu.make_async_remote_copy(
-            kv.at[i, :, pl.ds(start + half * HALF, HALF), :],
-            kv.at[i, :, pl.ds(land + half * HALF, HALF), :],
-            halo_ss.at[i, n, half], halo_rs.at[i, n, half],
+            kv.at[i, which, pl.ds(start + half * HALF, HALF), :],
+            kv.at[i, which, pl.ds(land + half * HALF, HALF), :],
+            halo_ss.at[i, n, half, which], halo_rs.at[i, n, half, which],
             device_id=(tm, s + RING if up else s - RING), device_id_type=MESH)
 
-    def relay_copy(i, up):
+    def relay_copy(i, up, which):
         start, land = (OWN_HIGH, HIGH_SLOTS) if up else (OWN_LOW, LOW_SLOTS)
         n = 0 if up else 1
         return pltpu.make_async_remote_copy(
-            kv.at[i, :, pl.ds(start + HALF, HALF), :], kv.at[i, :, pl.ds(land, HALF), :],
-            halo_ss.at[i, n, 1], relay_rs.at[i], device_id=(tm, near), device_id_type=MESH)
-
-    def pass_copy(i, up):
+            kv.at[i, which, pl.ds(start + HALF, HALF), :], kv.at[i, which, pl.ds(land, HALF), :],
+            halo_ss.at[i, n, 1, which], relay_rs.at[i, which],
+            device_id=(tm, near), device_id_type=MESH)
+
+    def pass_copy(i, up, which):
         start, land = (HIGH_SLOTS, LOW_SLOTS) if up else (LOW_SLOTS, HIGH_SLOTS)
         n = 0 if up else 1
         return pltpu.make_async_remote_copy(
-            kv.at[i, :, pl.ds(start, HALF), :], kv.at[i, :, pl.ds(land + HALF, HALF), :],
-            pass_ss.at[i], halo_rs.at[i, n, 1], device_id=(tm, far), device_id_type=MESH)
+            kv.at[i, which, pl.ds(start, HALF), :], kv.at[i, which, pl.ds(land + HALF, HALF), :],
+            pass_ss.at[i, which], halo_rs.at[i, n, 1, which],
+            device_id=(tm, far), device_id_type=MESH)
 
     def hand_on(i):
-        @pl.when(last_run)
-        def _():
-            relay_copy(i, True).wait_recv()
-            pass_copy(i, True).start()
-
-        @pl.when(first_run)
-        def _():
-            relay_copy(i, False).wait_recv()
-            pass_copy(i, False).start()
+        for up, here in ((True, last_run), (False, first_run)):
+            @pl.when(here)
+            def _(up=up):
+                for which in range(2):
+                    relay_copy(i, up, which).wait_recv()
+                    pass_copy(i, up, which).start()
 
     def o_copy(i, d):
         j = lax.rem(z + d, RING)
@@ -181,8 +180,8 @@
             stale_copy(i, d).start()
 
     def start_kv(i):
-        for d in (2, 1, 3, 0):
-            for which in range(2):
+        for which in range(2):
+            for d in (2, 1, 3, 0):
                 kv_copy(i, d, which).start()
 
     def start_q(i):
@@ -190,36 +189,25 @@
             q_copy(i, d).start()
 
     def halo(i):
-        for d in range(RING):
-            for which in range(2):
+        for which in range(2):
+            for d in range(RING):
                 if d == 0:
                     kv_copy(i, d, which).wait()
                 else:
                     kv_copy(i, d, which).wait_recv()
 
-        @pl.when(has_high)
-        def _():
-            halo_copy(i, True, 0).start()
-
-        @pl.when(has_low)
-        def _():
-            halo_copy(i, False, 0).start()
-
-        @pl.when(has_high & jnp.logical_not(mid_low))
-        def _():
-            halo_copy(i, True, 1).start()
-
-        @pl.when(has_low & jnp.logical_not(mid_high))
-        def _():
-            halo_copy(i, False, 1).start()
-
-        @pl.when(mid_low)
-        def _():
-            relay_copy(i, True).start()
-
-        @pl.when(mid_high)
-        def _():
-            relay_copy(i, False).start()
+            for up, there, mid in ((True, has_high, mid_low), (False, has_low, mid_high)):
+                @pl.when(mid)
+                def _(up=up, which=which):
+                    relay_copy(i, up, which).start()
+
+                @pl.when(there)
+                def _(up=up, which=which):
+                    halo_copy(i, up, 0, which).start()
+
+                @pl.when(there & jnp.logical_not(mid))
+                def _(up=up, which=which):
+                    halo_copy(i, up, 1, which).start()
 
     start_kv(0)
     start_q(0)
@@ -259,6 +247,7 @@
                 kv[i, which, pl.ds((RING + REACH) * ROWS + HALF, HALF), :] = jnp.zeros(
                     (HALF, HEAD_DIM), BF16)
 
+    halo(0)
     pltpu.make_async_copy(sk_hbm, staging.at[0], loc.at[1]).wait()
     pltpu.make_async_copy(sv_hbm, staging.at[1], loc.at[2]).wait()
     for d in (2, 1, 3, 0):
@@ -280,7 +269,6 @@
                     else:
                         stale_out[i, d - 1, which, :, place] = one
 
-    halo(0)
     start_stale(0)
     for d in range(1, RING):
         allow_copy(d).wait_recv()
@@ -349,40 +337,54 @@
         oh[i, z] = ob[i, pl.ds(pl.multiple_of(z * ROWS, ROWS), ROWS), :]
         lse_in[i, z] = lse_out[i, z]
 
+    def columns(owner, i):
+        head = owner * OWN_HEADS + i
+        return pl.ds(pl.multiple_of(head * HEAD_DIM, HEAD_DIM), HEAD_DIM)
+
+    def apart(i):
+        for d in range(1, GROUPS):
+            stale_copy(i, d).wait_recv()
+
+        @pl.loop(0, RING * ROWS // BLOCK)
+        def _(n):
+            owner = n // (ROWS // BLOCK)
+            b = n % (ROWS // BLOCK)
+            cols = columns(owner, i)
+            rows = pl.ds(pl.multiple_of(b * BLOCK, BLOCK), BLOCK)
+            place = pl.ds(pl.multiple_of(owner * HEAD_DIM, HEAD_DIM), HEAD_DIM)
+            x = scores(qh[rows, cols], stale[i, 0, :, place]) * FACTOR
+            m = jnp.max(x, axis=1, keepdims=True)
+            acc = with_sums(jnp.exp2(x - m).astype(BF16), stale[i, 1, :, place])
+            total = acc[:, HEAD_DIM:]
+            merged[rows, cols] = (acc[:, :HEAD_DIM] / total).astype(BF16)
+            lse = m + jnp.log2(total)
+            for tt in range(BLOCK // TILE):
+                turned = lse[tt * TILE:(tt + 1) * TILE, :].T
+                lse_st[i, owner, pl.ds(b * (BLOCK // TILE) + tt, 1), :] = turned[0:1, :]
+
+    def out_copy(i, owner):
+        cols = columns(owner, i)
+        return pltpu.make_async_copy(merged.at[:, cols], out_hbm.at[:, cols], out_sem.at[i, owner])
+
     def merge(i):
         for d in range(1, RING):
             o_copy(i, d).wait_recv()
             l_copy(i, d).wait_recv()
-            stale_copy(i, d).wait_recv()
-
-        @pl.loop(0, RING * ROWS // BLOCK)
-        def _(n):
-            owner = n // (ROWS // BLOCK)
-            b = n % (ROWS // BLOCK)
-            head = owner * OWN_HEADS + i
-            cols = pl.ds(pl.multiple_of(head * HEAD_DIM, HEAD_DIM), HEAD_DIM)
-            rows = pl.ds(pl.multiple_of(b * BLOCK, BLOCK), BLOCK)
-            place = pl.ds(pl.multiple_of(owner * HEAD_DIM, HEAD_DIM), HEAD_DIM)
-            x = scores(qh[rows, cols], stale[i, 0, :, place]) * FACTOR
-            lse = []
-            for tt in range(BLOCK // TILE):
-                one = lse_in[i, owner, pl.ds(b * (BLOCK // TILE) + tt, 1), :]
-                lse.append(jnp.broadcast_to(one, (TILE, TILE)).T)
-            lse = jnp.concatenate(lse, axis=0)
-            m = jnp.maximum(jnp.max(x, axis=1, keepdims=True), lse)
-            old = jnp.exp2(lse - m)
-            p = [jnp.exp2(x[:, k * TILE:(k + 1) * TILE] - m) for k in range(GROUPS)]
-            acc = with_sums(jnp.concatenate(p, axis=1).astype(BF16), stale[i, 1, :, place])
-            o = oh[i, owner, rows, :].astype(F32)
-            out_ref[rows, cols] = (
-                (old * o + acc[:, :HEAD_DIM]) / (old + acc[:, HEAD_DIM:])).astype(BF16)
+
+        @pl.loop(0, RING)
+        def _(owner):
+            cols = columns(owner, i)
+            for t in range(TILES_DEV):
+                rows = slice(t * TILE, (t + 1) * TILE)
+                share = 1 / (1 + jnp.exp2(lse_st[i, owner, t:t + 1, :] - lse_in[i, owner, t:t + 1, :]))
+                share = jnp.broadcast_to(share, (TILE, TILE)).T
+                old = merged[rows, cols].astype(F32)
+                new = oh[i, owner, rows, :].astype(F32)
+                merged[rows, cols] = (old + share * (new - old)).astype(BF16)
+            out_copy(i, owner).start()
 
     @pl.loop(0, OWN_HEADS)
     def _(i):
-        @pl.when(i < OWN_HEADS - 2)
-        def _():
-            pass
-
         @pl.when(i < OWN_HEADS - 1)
         def _():
             halo(i + 1)
@@ -391,6 +393,10 @@
         @pl.when(i == 0)
         def _():
             hand_on(0)
+
+        @pl.when(i > 0)
+        def _():
+            apart(i - 1)
 
         @pl.when(i == OWN_HEADS - 1)
         def _():
@@ -406,19 +412,23 @@
 
         @pl.when(has_low)
         def _():
-            halo_copy(i, True, 0).wait_recv()
-            halo_copy(i, True, 1).wait_recv()
+            for which in range(2):
+                halo_copy(i, True, 0, which).wait_recv()
+                halo_copy(i, True, 1, which).wait_recv()
 
         @pl.when(has_high)
         def _():
-            halo_copy(i, False, 0).wait_recv()
-            halo_copy(i, False, 1).wait_recv()
+            for which in range(2):
+                halo_copy(i, False, 0, which).wait_recv()
+                halo_copy(i, False, 1, which).wait_recv()
 
         fresh(i)
 
         @pl.when(i < OWN_HEADS - 1)
         def _():
             hand_on(i + 1)
+
+    apart(OWN_HEADS - 1)
 
     @pl.loop(EARLY, OWN_HEADS)
     def _(i):
@@ -429,27 +439,32 @@
 
     @pl.loop(0, OWN_HEADS)
     def _(i):
+        out_copy(i, 0).wait()
         for d in range(1, RING):
             for which in range(2):
                 kv_copy(i, d, which).wait_send()
             q_copy(i, d).wait_send()
             o_copy(i, d).wait_send()
             l_copy(i, d).wait_send()
+            out_copy(i, d).wait()
             stale_copy(i, d).wait_send()
 
         @pl.when(has_high)
         def _():
-            halo_copy(i, True, 0).wait_send()
-            halo_copy(i, True, 1).wait_send()
+            for which in range(2):
+                halo_copy(i, True, 0, which).wait_send()
+                halo_copy(i, True, 1, which).wait_send()
 
         @pl.when(has_low)
         def _():
-            halo_copy(i, False, 0).wait_send()
-            halo_copy(i, False, 1).wait_send()
+            for which in range(2):
+                halo_copy(i, False, 0, which).wait_send()
+                halo_copy(i, False, 1, which).wait_send()
 
         @pl.when(last_run | first_run)
         def _():
-            pass_copy(i, True).wait_send()
+            for which in range(2):
+                pass_copy(i, True, which).wait_send()
 
 
 def body(queries, keys, values, stale_keys, stale_values, tile_mask, stale_pick):
@@ -460,7 +475,7 @@
         kernel,
         out_shape=jax.ShapeDtypeStruct((ROWS, WIDTH), BF16),
         in_specs=[hbm] * 5 + [smem] * 2,
-        out_specs=pl.BlockSpec(memory_space=pltpu.VMEM),
+        out_specs=hbm,
         scratch_shapes=[
             pltpu.VMEM((OWN_HEADS, 2, SLOTS * ROWS, HEAD_DIM), BF16),
             pltpu.VMEM((OWN_HEADS, RING * ROWS, HEAD_DIM), BF16),
@@ -475,15 +490,18 @@
             pltpu.VMEM((BLOCK, TILE), F32), pltpu.VMEM((BLOCK, TILE), F32),
             pltpu.VMEM((OWN_HEADS, RING, 8, TILE), F32),
             pltpu.VMEM((OWN_HEADS, RING, 8, TILE), F32),
+            pltpu.VMEM((OWN_HEADS, RING, 8, TILE), F32),
+            pltpu.VMEM((ROWS, WIDTH), BF16),
             dma((OWN_HEADS, RING, 2)), dma((OWN_HEADS, RING, 2)),
             dma((OWN_HEADS, RING)), dma((OWN_HEADS, RING)),
-            dma((OWN_HEADS, 2, 2)), dma((OWN_HEADS, 2, 2)),
-            dma((OWN_HEADS,)), dma((OWN_HEADS,)),
+            dma((OWN_HEADS, 2, 2, 2)), dma((OWN_HEADS, 2, 2, 2)),
+            dma((OWN_HEADS, 2)), dma((OWN_HEADS, 2)),
             dma((OWN_HEADS, RING)), dma((OWN_HEADS, RING)),
             dma((OWN_HEADS, RING)), dma((OWN_HEADS, RING)),
             dma((RING,)), dma((RING,)),
             dma((OWN_HEADS, GROUPS)), dma((OWN_HEADS, GROUPS)),
             dma((3,)),
+            dma((OWN_HEADS, RING)),
         ],
         compiler_params=pltpu.CompilerParams(
             collective_id=0, has_side_effects=True, vmem_limit_bytes=58 * 2**20

time: 181 us -> 164 us (0.906)
  Pallas kernels: 175 us -> 160 us
    pallas_call x1, Pallas kernels: 175 us -> 160 us  [body(): pl.pallas_call(kernel, out_shape=jax.ShapeDtypeStruct((ROWS, WIDTH), BF16...]
where the time goes in v4:
time: 164 us
  Pallas kernels  160 us (98%)
  local copies, waits for them, and re-layouts  3.76 us (2%)
    pallas_call x1, Pallas kernels, body(): pl.pallas_call(kernel, out_shape=jax.ShapeDtypeStruct((ROWS, WIDTH), BF16...  160 us
    unnamed x1, local copies, waits for them, and re-layouts  3.76 us

profile of v4, /device:TPU:1, one launch (start us, length us, event | category | flops | bytes accessed | tf_op | source)
XLA Modules:
  0.0 163.5 jit_solution(10374947158616084811)
XLA Ops:
  0.0 159.7 %shard_map.73 = bf16[512,3072]{1,0:T(8,128)(2,1)} custom-call(bf16[512,3072]{1,0:T(8,128)(2,1)} %q_hbm.1, bf16[512,3072]{1,0:T(8,128)(2,1)} %k_hbm.1, bf16[512,3072]{1,0:T(8,128)(2,1)} %v_hbm.1, bf16[512,3072]{1,0:T(8,128)(2,1)} %sk_hbm.1, bf16[512,3072]{1,0:T(8,128)(2,1)} %sv_hbm.1, s32[4,4,7]{2,1,0:T(4,128)} %bitcast.1, s32[1,4]{1,0:T(1,128)} %pick_ref.1), custom_call_target="tpu_custom_call" | custom-call | flops 25769803776 | bytes 25165824 | tf_op jit(solution)/shard_map/pallas_call | solution.py:474
  159.7 3.8 %copy.9 = bf16[512,3072]{1,0:T(8,128)(2,1)} copy(bf16[512,3072]{1,0:T(8,128)(2,1)} %shard_map.73) | data formatting | bytes 6291456

commit v5 on v4

--- a/solution.py
+++ b/solution.py
@@ -46,7 +46,7 @@
 
 def kernel(
     q_hbm, k_hbm, v_hbm, sk_hbm, sv_hbm, mask_ref, pick_ref, out_hbm,
-    kv, qr, ob, oh, stale, stale_out, staging, qh, allow, sc_a, sc_b, top_a, top_b, lse_out, lse_in, lse_st, merged,
+    kv, qr, ob, oh, stale, stale_out, staging, qh, allow, sc_a, sc_b, top_a, top_b, lse_out, lse_in, lse_st, merged, packed,
     kv_ss, kv_rs, q_ss, q_rs, halo_ss, halo_rs, relay_rs, pass_ss, o_ss, o_rs, l_ss, l_rs,
     a_ss, a_rs, st_ss, st_rs, loc, out_sem,
 ):
@@ -120,7 +120,7 @@
 
     def allow_copy(d):
         return pltpu.make_async_remote_copy(
-            allow.at[z], allow.at[z], a_ss.at[d], a_rs.at[d],
+            packed.at[z], packed.at[z], a_ss.at[d], a_rs.at[d],
             device_id=ring(d), device_id_type=MESH)
 
     LOW_SLOTS, OWN_LOW, OWN_HIGH, HIGH_SLOTS = 0, REACH * ROWS, RING * ROWS, (RING + REACH) * ROWS
@@ -188,32 +188,31 @@
         for d in (2, 1, 3, 0):
             q_copy(i, d).start()
 
-    def halo(i):
-        for which in range(2):
-            for d in range(RING):
-                if d == 0:
-                    kv_copy(i, d, which).wait()
-                else:
-                    kv_copy(i, d, which).wait_recv()
-
-            for up, there, mid in ((True, has_high, mid_low), (False, has_low, mid_high)):
-                @pl.when(mid)
-                def _(up=up, which=which):
-                    relay_copy(i, up, which).start()
-
-                @pl.when(there)
-                def _(up=up, which=which):
-                    halo_copy(i, up, 0, which).start()
-
-                @pl.when(there & jnp.logical_not(mid))
-                def _(up=up, which=which):
-                    halo_copy(i, up, 1, which).start()
+    def halo(i, which):
+        for d in range(RING):
+            if d == 0:
+                kv_copy(i, d, which).wait()
+            else:
+                kv_copy(i, d, which).wait_recv()
+
+        for up, there, mid in ((True, has_high, mid_low), (False, has_low, mid_high)):
+            @pl.when(mid)
+            def _(up=up):
+                relay_copy(i, up, which).start()
+
+            @pl.when(there)
+            def _(up=up):
+                halo_copy(i, up, 0, which).start()
+
+            @pl.when(there & jnp.logical_not(mid))
+            def _(up=up):
+                halo_copy(i, up, 1, which).start()
 
     start_kv(0)
     start_q(0)
-    pltpu.make_async_copy(q_hbm, qh, loc.at[0]).start()
     pltpu.make_async_copy(sk_hbm, staging.at[0], loc.at[1]).start()
     pltpu.make_async_copy(sv_hbm, staging.at[1], loc.at[2]).start()
+    pltpu.make_async_copy(q_hbm, qh, loc.at[0]).start()
 
     for t in range(TILES_DEV):
         for o in range(WINDOW):
@@ -224,6 +223,9 @@
                 else:
                     value = jnp.full((1, TILE), mask_ref[t, j, o], jnp.int32).astype(F32) * there
                 allow[z, pl.ds(t * 32 + o * TILES_DEV + j, 1), :] = value
+    for t in range(TILES_DEV):
+        allow[z, pl.ds(t * 32 + 28, 4), :] = jnp.zeros((4, TILE), F32)
+    packed[z] = allow[z].T[0:8, :]
     for d in range(1, RING):
         allow_copy(d).start()
 
@@ -247,7 +249,7 @@
                 kv[i, which, pl.ds((RING + REACH) * ROWS + HALF, HALF), :] = jnp.zeros(
                     (HALF, HEAD_DIM), BF16)
 
-    halo(0)
+    halo(0, 0)
     pltpu.make_async_copy(sk_hbm, staging.at[0], loc.at[1]).wait()
     pltpu.make_async_copy(sv_hbm, staging.at[1], loc.at[2]).wait()
     for d in (2, 1, 3, 0):
@@ -270,8 +272,11 @@
                         stale_out[i, d - 1, which, :, place] = one
 
     start_stale(0)
+    halo(0, 1)
     for d in range(1, RING):
         allow_copy(d).wait_recv()
+        j = lax.rem(z + RING - d, RING)
+        allow[j] = jnp.broadcast_to(packed[j, 0:1, :], (TILE, TILE)).T
     pltpu.make_async_copy(q_hbm, qh, loc.at[0]).wait()
 
     def both(i, scored, weighed):
@@ -387,7 +392,8 @@
     def _(i):
         @pl.when(i < OWN_HEADS - 1)
         def _():
-            halo(i + 1)
+            halo(i + 1, 0)
+            halo(i + 1, 1)
             start_stale(i + 1)
 
         @pl.when(i == 0)
@@ -428,10 +434,12 @@
         def _():
             hand_on(i + 1)
 
-    apart(OWN_HEADS - 1)
-
     @pl.loop(EARLY, OWN_HEADS)
     def _(i):
+        @pl.when(i == OWN_HEADS - 1)
+        def _():
+            apart(i)
+
         merge(i)
 
     for d in range(1, RING):
@@ -492,6 +500,7 @@
             pltpu.VMEM((OWN_HEADS, RING, 8, TILE), F32),
             pltpu.VMEM((OWN_HEADS, RING, 8, TILE), F32),
             pltpu.VMEM((ROWS, WIDTH), BF16),
+            pltpu.VMEM((RING, 8, TILE), F32),
             dma((OWN_HEADS, RING, 2)), dma((OWN_HEADS, RING, 2)),
             dma((OWN_HEADS, RING)), dma((OWN_HEADS, RING)),
             dma((OWN_HEADS, 2, 2, 2)), dma((OWN_HEADS, 2, 2, 2)),

time: 164 us -> 162 us (0.988)
  Pallas kernels: 160 us -> 158 us
    pallas_call x1, Pallas kernels: 160 us -> 158 us  [body(): pl.pallas_call(kernel, out_shape=jax.ShapeDtypeStruct((ROWS, WIDTH), BF16...]
where the time goes in v5:
time: 162 us
  Pallas kernels  158 us (98%)
  local copies, waits for them, and re-layouts  3.76 us (2%)
    pallas_call x1, Pallas kernels, body(): pl.pallas_call(kernel, out_shape=jax.ShapeDtypeStruct((ROWS, WIDTH), BF16...  158 us
    unnamed x1, local copies, waits for them, and re-layouts  3.76 us

profile of v5, /device:TPU:1, one launch (start us, length us, event | category | flops | bytes accessed | tf_op | source)
XLA Modules:
  0.0 161.6 jit_solution(13409894513555888699)
XLA Ops:
  0.0 157.8 %shard_map.73 = bf16[512,3072]{1,0:T(8,128)(2,1)} custom-call(bf16[512,3072]{1,0:T(8,128)(2,1)} %q_hbm.1, bf16[512,3072]{1,0:T(8,128)(2,1)} %k_hbm.1, bf16[512,3072]{1,0:T(8,128)(2,1)} %v_hbm.1, bf16[512,3072]{1,0:T(8,128)(2,1)} %sk_hbm.1, bf16[512,3072]{1,0:T(8,128)(2,1)} %sv_hbm.1, s32[4,4,7]{2,1,0:T(4,128)} %bitcast.1, s32[1,4]{1,0:T(1,128)} %pick_ref.1), custom_call_target="tpu_custom_call" | custom-call | flops 25769803776 | bytes 25165824 | tf_op jit(solution)/shard_map/pallas_call | solution.py:482
  157.8 3.8 %copy.9 = bf16[512,3072]{1,0:T(8,128)(2,1)} copy(bf16[512,3072]{1,0:T(8,128)(2,1)} %shard_map.73) | data formatting | bytes 6291456
